TPU v7x, 512 devices: a whole 4x4x16 slice. The times are simulated.
512 devices in a mesh: gx: 8 (over x, z_hi), gy: 8 (over y, core), gz: 8 (over z_lo).
Axes of the slice: x: 4, y: 4, z: 16 (z_hi: 2, z_lo: 8; z = z_hi * 8 + z_lo), core: 2. Of those that a mesh axis runs over, the one named last changes fastest.
Arguments:
- tokens: bfloat16 [1024, 8192], P('gx', ('gz', 'gy')), may hold values from -6 to 6
- cotangent: bfloat16 [1024, 8192], P('gx', ('gz', 'gy')), may hold values from -6 to 6
- gate_weight: bfloat16 [8192, 14336], P(('gz', 'gx'), 'gy'), may hold values from -0.0625 to 0.0625
- up_weight: bfloat16 [8192, 14336], P(('gz', 'gx'), 'gy'), may hold values from -0.0625 to 0.0625
- down_weight: bfloat16 [14336, 8192], P('gy', ('gz', 'gx')), may hold values from -0.046875 to 0.046875
Outputs:
- output: bfloat16 [1024, 8192], P('gx', ('gz', 'gy'))
- input_grad: bfloat16 [1024, 8192], P('gx', ('gz', 'gy'))
- gate_grad: bfloat16 [8192, 14336], P('gz', ('gy', 'gx'))
- up_grad: bfloat16 [8192, 14336], P('gz', ('gy', 'gx'))
- down_grad: bfloat16 [14336, 8192], P(('gy', 'gx'), 'gz')
All inputs are finite; a program needn't handle non-finite values.
Results may differ from a plain program's by a relative error of at most 0.0049.
Values may be sent and summed in bfloat16 or wider, within the bound.
No kernel may reach another device: no remote copies, remote signals or barrier semaphores. Data moves between devices by JAX's collectives and lax.ppermute only.
A program may use at most 64 MiB of HBM per device.

v0:
```python
import jax
import jax.numpy as jnp
from jax import lax
from jax.sharding import PartitionSpec as P


def contract_rows(left, right):
    return lax.dot_general(
        left, right, (((0,), (0,)), ((), ())), preferred_element_type=jnp.float32
    )


def contract_cols(left, right):
    return lax.dot_general(
        left, right, (((1,), (1,)), ((), ())), preferred_element_type=jnp.float32
    )


def per_device(tokens, cotangent, gate_weight, up_weight, down_weight):
    feat_block, grad_block = (
        lax.all_gather(tokens, "gy", axis=1, tiled=True),
        lax.all_gather(cotangent, "gy", axis=1, tiled=True),
    )
    gate_tile, up_tile, down_tile = (
        lax.all_gather(gate_weight, "gx", axis=0, tiled=True),
        lax.all_gather(up_weight, "gx", axis=0, tiled=True),
        lax.all_gather(down_weight, "gx", axis=1, tiled=True),
    )
    gate_part = jnp.dot(feat_block, gate_tile, preferred_element_type=jnp.float32)
    upper_part = jnp.dot(feat_block, up_tile, preferred_element_type=jnp.float32)
    hidden_part = contract_cols(grad_block, down_tile)
    gate, upper = lax.psum((gate_part, upper_part), "gz")
    sigma = jax.nn.sigmoid(gate)
    activated = gate * sigma
    hidden = (activated * upper).astype(jnp.bfloat16)
    hidden_grad = lax.psum(hidden_part, "gz")
    gate_delta = (hidden_grad * upper * sigma * (1.0 + gate * (1.0 - sigma))).astype(jnp.bfloat16)
    up_delta = (hidden_grad * activated).astype(jnp.bfloat16)
    output_part = jnp.dot(hidden, down_tile, preferred_element_type=jnp.float32)
    input_part = contract_cols(gate_delta, gate_tile) + contract_cols(up_delta, up_tile)
    output, input_grad = (
        lax.psum_scatter(output_part, "gy", scatter_dimension=1, tiled=True),
        lax.psum_scatter(input_part, "gy", scatter_dimension=1, tiled=True),
    )
    hidden_cols, gate_cols, up_cols = (
        lax.all_to_all(hidden, "gx", split_axis=1, concat_axis=0, tiled=True),
        lax.all_to_all(gate_delta, "gx", split_axis=1, concat_axis=0, tiled=True),
        lax.all_to_all(up_delta, "gx", split_axis=1, concat_axis=0, tiled=True),
    )
    feat_piece = lax.all_gather(feat_block, "gx", axis=0, tiled=True)
    grad_piece = lax.all_gather(grad_block, "gx", axis=0, tiled=True)
    down_grad = contract_rows(hidden_cols, grad_piece)
    gate_grad = contract_rows(feat_piece, gate_cols)
    up_grad = contract_rows(feat_piece, up_cols)
    return (
        output.astype(jnp.bfloat16),
        input_grad.astype(jnp.bfloat16),
        gate_grad.astype(jnp.bfloat16),
        up_grad.astype(jnp.bfloat16),
        down_grad.astype(jnp.bfloat16),
    )


def solution(mesh):
    placed = (
        P("gx", ("gz", "gy")),
        P("gx", ("gz", "gy")),
        P(("gz", "gx"), "gy"),
        P(("gz", "gx"), "gy"),
        P("gy", ("gz", "gx")),
    )
    return jax.shard_map(
        per_device,
        mesh=mesh,
        in_specs=placed,
        out_specs=(
            P("gx", ("gz", "gy")),
            P("gx", ("gz", "gy")),
            P("gz", ("gy", "gx")),
            P("gz", ("gy", "gx")),
            P(("gy", "gx"), "gz"),
        ),
        check_vma=False,
    )
```

profile of v0, /device:TPU:1, one launch (start us, length us, event | category | flops | bytes accessed | tf_op | source)
XLA Modules:
  0.0 974.5 jit_solution(6399603521075452841)
XLA Ops:
  9.4 18.4 %all_gather.21 = bf16[128,1024]{1,0:T(8,128)(2,1)S(1)} all-gather(bf16[128,128]{1,0:T(8,128)(2,1)} %param.5), channel_id=1, replica_groups=mesh['gx'=8,'gy'=8,'gz'=8] {'gy'}, dimensions={1}, use_global_device_ids=true | all-gather | bytes 294912 | tf_op jit(solution)/shard_map/all_gather | solution.py:21
  27.9 11.9 %all_gather.25 = bf16[128,1024]{1,0:T(8,128)(2,1)S(1)} all-gather(bf16[128,128]{1,0:T(8,128)(2,1)} %param.6), channel_id=1, replica_groups=mesh['gx'=8,'gy'=8,'gz'=8] {'gy'}, dimensions={1}, use_global_device_ids=true | all-gather | bytes 294912 | tf_op jit(solution)/shard_map/all_gather | solution.py:22
  39.7 136.5 %all-gather.8.cloned.1.call-done = bf16[1024,1792]{1,0:T(8,128)(2,1)} async-done(((bf16[128,1792]{1,0:T(8,128)(2,1)}), bf16[1024,1792]{1,0:T(8,128)(2,1)}) %all-gather.8.cloned.1.call-update) | async-done | bytes 3670032 | tf_op jit(solution)/shard_map/all_gather | solution.py:26
  176.3 3.6 fusion.10
  179.9 153.7 %all-gather.6.cloned.1.call-done = bf16[1024,1792]{1,0:T(8,128)(2,1)} async-done(((bf16[128,1792]{1,0:T(8,128)(2,1)}), bf16[1024,1792]{1,0:T(8,128)(2,1)}) %all-gather.6.cloned.1.call-update) | async-done | bytes 3670032 | tf_op jit(solution)/shard_map/all_gather | solution.py:25
  333.6 3.6 fusion.9
  337.2 158.4 %all-gather.10.cloned.1.call-done = bf16[1792,1024]{1,0:T(8,128)(2,1)} async-done(((bf16[1792,128]{1,0:T(8,128)(2,1)}), bf16[1792,1024]{1,0:T(8,128)(2,1)}) %all-gather.10.cloned.1.call-update) | async-done | bytes 3670032 | tf_op jit(solution)/shard_map/all_gather | solution.py:27
  495.6 4.3 fusion.12
  500.0 147.9 %all-reduce.3.cloned.1.call-done = (f32[128,1792]{1,0:T(8,128)}, f32[128,1792]{1,0:T(8,128)}, f32[128,1792]{1,0:T(8,128)}) async-done(((f32[128,1792]{1,0:T(8,128)}, f32[128,1792]{1,0:T(8,128)}, f32[128,1792]{1,0:T(8,128)}), (f32[128,1792]{1,0:T(8,128)}, f32[128,1792]{1,0:T(8,128)}, f32[128,1792]{1,0:T(8,128)})) %all-reduce.3.cloned.1.call-update) | async-done | bytes 2752528 | tf_op jit(solution)/shard_map/psum | solution.py:32
  647.9 2.4 multiply_convert_fusion
  652.1 2.1 convolution_add_fusion
  654.3 3.5 fusion.11
  659.5 7.8 all-to-all-start
  669.1 14.8 %all-to-all-done = bf16[128,8,224]{0,2,1:T(8,128)(2,1)S(1)} async-done(((bf16[128,8,224]{0,2,1:T(8,128)(2,1)}), bf16[128,8,224]{0,2,1:T(8,128)(2,1)S(1)}, u32[]{:S(2)}, u32[]{:S(2)}) %all-to-all-start) | async-done | bytes 458784 | tf_op jit(solution)/shard_map/all_to_all | solution.py:47
  683.9 3.5 all-to-all-start.1
  688.4 15.0 %all-to-all-done.1 = bf16[128,8,224]{0,2,1:T(8,128)(2,1)S(1)} async-done(((bf16[128,8,224]{0,2,1:T(8,128)(2,1)}), bf16[128,8,224]{0,2,1:T(8,128)(2,1)S(1)}, u32[]{:S(2)}, u32[]{:S(2)}) %all-to-all-start.1) | async-done | bytes 458784 | tf_op jit(solution)/shard_map/all_to_all | solution.py:48
  703.4 4.2 all-to-all-start.2
  707.6 1.5 convert_element_type.34
  709.0 19.2 %reduce-scatter.3.cloned.1.call-done = f32[128,128]{1,0:T(8,128)} async-done(((f32[128,1024]{1,0:T(8,128)}), f32[128,128]{1,0:T(8,128)}) %reduce-scatter.3.cloned.1.call-update) | async-done | bytes 65552 | tf_op jit(solution)/shard_map/reduce_scatter | solution.py:42
  729.7 120.0 %all-gather.12.cloned.1.call-done = bf16[1024,1024]{1,0:T(8,128)(2,1)} async-done(((bf16[128,1024]{1,0:T(8,128)(2,1)}), bf16[1024,1024]{1,0:T(8,128)(2,1)}) %all-gather.12.cloned.1.call-update) | async-done | bytes 2097168 | tf_op jit(solution)/shard_map/all_gather | solution.py:50
  849.7 3.0 fusion
  852.7 3.0 fusion.1
  855.7 108.9 %all-gather.14.cloned.1.call-done = bf16[1024,1024]{1,0:T(8,128)(2,1)} async-done(((bf16[128,1024]{1,0:T(8,128)(2,1)}), bf16[1024,1024]{1,0:T(8,128)(2,1)}) %all-gather.14.cloned.1.call-update) | async-done | bytes 2097168 | tf_op jit(solution)/shard_map/all_gather | solution.py:51
  964.6 3.0 convolution_convert_fusion
  (31 shorter events, 10.0 us)
Async XLA Ops:
  7.2 169.1 %all-gather.8.cloned.1.call-start = ((), (), s32[]{:S(2)}) async-start(), calls=%async_computation.6 | async-start | bytes 4128768 | tf_op jit(solution)/shard_map/all_gather | solution.py:26
  7.9 325.7 %all-gather.6.cloned.1.call-start = ((), (), s32[]{:S(2)}) async-start(), calls=%async_computation.5 | async-start | bytes 4128768 | tf_op jit(solution)/shard_map/all_gather | solution.py:25
  8.6 487.0 %all-gather.10.cloned.1.call-start = ((), (), s32[]{:S(2)}) async-start(), calls=%async_computation.7 | async-start | bytes 4128768 | tf_op jit(solution)/shard_map/all_gather | solution.py:27
  9.4 638.5 %all-reduce.3.cloned.1.call-start = ((), (), s32[]{:S(2)}) async-start(), calls=%async_computation.12 | async-start | bytes 5505024 | tf_op jit(solution)/shard_map/psum | solution.py:32
  27.9 309.3 %copy-start.2 = (bf16[128,1024]{1,0:T(8,128)(2,1)}, bf16[128,1024]{1,0:T(8,128)(2,1)S(1)}, u32[]{:S(2)}) copy-start(bf16[128,1024]{1,0:T(8,128)(2,1)S(1)} %all_gather.21) | copy-start | bytes 786436
  39.7 455.9 %copy-start.3 = (bf16[128,1024]{1,0:T(8,128)(2,1)}, bf16[128,1024]{1,0:T(8,128)(2,1)S(1)}, u32[]{:S(2)}) copy-start(bf16[128,1024]{1,0:T(8,128)(2,1)S(1)} %all_gather.25) | copy-start | bytes 786436
  500.0 207.6 %reduce-scatter.5.cloned.1.call-start = ((), (), s32[]{:S(2)}) async-start(), calls=%async_computation.9 | async-start | bytes 589824 | tf_op jit(solution)/shard_map/reduce_scatter | solution.py:43
  647.9 2.9 copy-start.1
  647.9 4.2 copy-start
  654.2 74.0 %reduce-scatter.3.cloned.1.call-start = ((), (), s32[]{:S(2)}) async-start(), calls=%async_computation.8 | async-start | bytes 589824 | tf_op jit(solution)/shard_map/reduce_scatter | solution.py:42
  657.8 191.9 %all-gather.12.cloned.1.call-start = ((), (), s32[]{:S(2)}) async-start(), calls=%async_computation.10 | async-start | bytes 2359296 | tf_op jit(solution)/shard_map/all_gather | solution.py:50
  659.5 24.4 %all-to-all-start = ((bf16[128,8,224]{0,2,1:T(8,128)(2,1)}), bf16[128,8,224]{0,2,1:T(8,128)(2,1)S(1)}, u32[]{:S(2)}, u32[]{:S(2)}) async-start(bf16[128,8,224]{0,2,1:T(8,128)(2,1)} %bitcast), calls=%async_computation.2 | async-start | bytes 917504 | tf_op jit(solution)/shard_map/all_to_all | solution.py:47
  667.3 297.3 %all-gather.14.cloned.1.call-start = ((), (), s32[]{:S(2)}) async-start(), calls=%async_computation.11 | async-start | bytes 2359296 | tf_op jit(solution)/shard_map/all_gather | solution.py:51
  683.9 19.5 %all-to-all-start.1 = ((bf16[128,8,224]{0,2,1:T(8,128)(2,1)}), bf16[128,8,224]{0,2,1:T(8,128)(2,1)S(1)}, u32[]{:S(2)}, u32[]{:S(2)}) async-start(bf16[128,8,224]{0,2,1:T(8,128)(2,1)} %bitcast.3), calls=%async_computation.3 | async-start | bytes 917504 | tf_op jit(solution)/shard_map/all_to_all | solution.py:48
  703.4 261.2 %all-to-all-start.2 = ((bf16[128,8,224]{0,2,1:T(8,128)(2,1)}), bf16[128,8,224]{0,2,1:T(8,128)(2,1)S(1)}, u32[]{:S(2)}, u32[]{:S(2)}) async-start(bf16[128,8,224]{0,2,1:T(8,128)(2,1)} %bitcast.6), calls=%async_computation.4 | async-start | bytes 917504 | tf_op jit(solution)/shard_map/all_to_all | solution.py:46
Sparse Core Ops, SparseCore 0:
  11.2 165.0 all-gather.7
  179.4 154.0 all-gather.5
  336.6 158.9 all-gather.9
  500.1 147.7 all-reduce.2
  654.4 33.2 reduce-scatter.4
  690.3 37.8 reduce-scatter.2
  732.5 117.1 all-gather.11
  853.4 111.1 all-gather.13
where the time goes:
time: 976 us; the launch traced here: 974 us
  waiting for transfers between devices  878 us (90%)
  blocking collectives  30.3 us (3%)
  matrix products  27.5 us (3%)
  starting transfers between devices  15.7 us (2%)
  between operations  14.2 us (1%)
    all_gather x1, waiting for transfers between devices, per_device(): lax.all_gather(down_weight, 'gx', axis=1, tiled=True)  158 us
    all_gather x1, waiting for transfers between devices, per_device(): lax.all_gather(gate_weight, 'gx', axis=0, tiled=True)  154 us
    psum x1, waiting for transfers between devices, per_device(): gate, upper = lax.psum((gate_part, upper_part), 'gz')  148 us
    all_gather x1, waiting for transfers between devices, per_device(): lax.all_gather(up_weight, 'gx', axis=0, tiled=True)  137 us
    all_gather x1, waiting for transfers between devices, per_device(): feat_piece = lax.all_gather(feat_block, 'gx', axis=0, tiled=True)  120 us
    all_gather x1, waiting for transfers between devices, per_device(): grad_piece = lax.all_gather(grad_block, 'gx', axis=0, tiled=True)  109 us
  transfers between devices with their start and end apart: 11, of which 9 were waited for; matrix products, arithmetic and copies ran while one was open for 2% of the time, Pallas kernels for 0%

commit v1 on v0

v1 whole, which is shorter than its diff:
```python
import jax
import jax.numpy as jnp
from jax import lax
from jax.sharding import Mesh, PartitionSpec as P

BF = jnp.bfloat16
F32 = jnp.float32
WIRE = jnp.bfloat16
DEPTH = ("zh", "gz")


def dot(left, right, left_dim, right_dim):
    return lax.dot_general(
        left, right, (((left_dim,), (right_dim,)), ((), ())), preferred_element_type=F32
    )


def swap(value, axis):
    return lax.ppermute(value, axis, [(0, 1), (1, 0)])


def shift(value, by):
    return lax.ppermute(value, DEPTH, [(i, (i + by) % 16) for i in range(16)])


def ordered(own, other, index):
    first = index == 0
    return jnp.stack([jnp.where(first, own, other), jnp.where(first, other, own)])


def take(value, index, dim=0):
    return lax.dynamic_index_in_dim(value, index, dim, keepdims=False)


def gather_plane(both):
    core = lax.axis_index("c")
    both = jnp.broadcast_to(both[None], (16,) + both.shape)
    own = lax.all_to_all(both, ("x", "y"), 0, 0, tiled=True)
    own = own.reshape((4, 4) + own.shape[1:])
    pair = ordered(own, swap(own, "c"), core)
    return pair.transpose(3, 1, 0, 4, 2, 5)


def per_device(tokens, cotangent, gate_weight, up_weight, down_weight):
    zh, core = lax.axis_index("zh"), lax.axis_index("c")
    level = lax.axis_index(DEPTH)
    tok, feat = tokens.shape
    cols = gate_weight.shape[1] // 4

    both = jnp.stack([tokens, cotangent])
    near = lax.ppermute(both, ("zh", "c"), [(0, 0), (1, 2), (2, 1), (3, 3)])
    far = lax.ppermute(both, ("zh", "c"), [(0, 2), (1, 0), (2, 3), (3, 1)])

    gate_up = jnp.concatenate(
        [gate_weight.reshape(tok, 4, cols), up_weight.reshape(tok, 4, cols)], axis=2
    )
    gate_up = lax.all_to_all(gate_up, "x", 1, 0).reshape(4 * tok, 2 * cols)
    down = lax.all_to_all(down_weight, "x", 0, 1, tiled=True)

    near = gather_plane(near)
    far = gather_plane(far)
    whole = ordered(near, far, zh)
    whole = whole.transpose(1, 2, 3, 4, 5, 0, 6).reshape(2, 8 * tok, 8 * feat)

    blocks = near.reshape(2, 4, 4, tok // 2, 4 * feat)

    def partial(by):
        rows = take(blocks, lax.rem(level + by + 16, 4), 2).reshape(2, 2 * tok, 4 * feat)
        return jnp.concatenate(
            [dot(rows[0], gate_up, 1, 0), dot(rows[1], down, 1, 1)], axis=1
        ).reshape(4, tok // 2, 3 * cols)

    across = partial(2).astype(WIRE)
    upward = shift(across[:2], 2)
    downward = shift(across[2:], -2)
    after = shift(partial(1).astype(WIRE), 1)
    before = shift(partial(-1).astype(WIRE), -1)
    part = partial(0)
    part = part + after.astype(F32) + before.astype(F32)
    part = part + jnp.concatenate([upward, downward]).astype(F32)
    row = level // 4

    def owed(by):
        return shift(take(part, lax.rem(row + by + 4, 4)).astype(WIRE), 4 * by)

    total = owed(2).astype(F32) + owed(1).astype(F32) + owed(-1).astype(F32)
    total = total + take(part, row)

    gate, upper, hidden_grad = (total[:, i * cols : (i + 1) * cols] for i in range(3))
    sigma = jax.nn.sigmoid(gate)
    activated = gate * sigma
    hidden = (activated * upper).astype(BF)
    gate_delta = (hidden_grad * upper * sigma * (1.0 + gate * (1.0 - sigma))).astype(BF)
    up_delta = (hidden_grad * activated).astype(BF)
    mine = jnp.concatenate([gate_delta, up_delta, hidden], axis=1)

    quarter = jnp.zeros((4,) + mine.shape, BF)
    quarter = lax.dynamic_update_index_in_dim(quarter, mine, row, 0)
    for by in (2, 1, -1):
        quarter = lax.dynamic_update_index_in_dim(
            quarter, shift(mine, 4 * by), lax.rem(row - by + 4, 4), 0
        )
    all_of = jnp.zeros((4,) + quarter.shape, BF)

    def put(buffer, value, by, start=0):
        at = lax.rem(level - by + 16, 4)
        return lax.dynamic_update_slice(buffer, value[:, None], (start, at, 0, 0))

    all_of = put(all_of, quarter, 0)
    all_of = put(all_of, shift(quarter, 1), 1)
    all_of = put(all_of, shift(quarter, -1), -1)
    all_of = put(all_of, shift(quarter[:2], 2), 2)
    all_of = put(all_of, shift(quarter[2:], -2), 2, 2)

    by_zh = all_of.reshape(4, 2, tok, 3 * cols)

    def parts(which):
        rows = take(by_zh, which, 1).reshape(4 * tok, 3 * cols)
        return jnp.stack(
            [dot(rows[:, 2 * cols :], down, 1, 0), dot(rows[:, : 2 * cols], gate_up, 1, 1)]
        )

    got = swap(parts(1 - core), "c")
    sums = (parts(core) + got).astype(BF)
    sums = sums.reshape(2, 4, tok, 4, feat).transpose(1, 3, 0, 2, 4)
    sums = lax.all_to_all(
        sums.reshape(16, 2, tok, feat), ("x", "y"), 0, 0, tiled=True
    )
    result = jnp.sum(sums.astype(F32), axis=0).astype(BF)
    result = lax.ppermute(result, ("zh", "c"), [(0, 0), (1, 2), (2, 1), (3, 3)])

    every = all_of.reshape(8 * tok, 3 * cols)
    half = cols // 2

    def own_half(at):
        return jnp.where(
            zh == 0, every[:, at : at + half], every[:, at + half : at + cols]
        )

    gate_grad = dot(whole[0], own_half(0), 0, 0)
    up_grad = dot(whole[0], own_half(cols), 0, 0)
    down_grad = dot(own_half(2 * cols), whole[1], 0, 0)
    return (
        result[0],
        result[1],
        gate_grad.astype(BF),
        up_grad.astype(BF),
        down_grad.astype(BF),
    )


def solution(mesh):
    fine = Mesh(mesh.devices.reshape(4, 2, 4, 2, 8), ("x", "zh", "y", "c", "gz"))
    gx, gy = ("x", "zh"), ("y", "c")
    act = P(gx, ("gz",) + gy)
    return jax.shard_map(
        per_device,
        mesh=fine,
        in_specs=(act, act, P(("gz",) + gx, gy), P(("gz",) + gx, gy), P(gy, ("gz",) + gx)),
        out_specs=(act, act, P("gz", gy + gx), P("gz", gy + gx), P(gy + gx, "gz")),
        check_vma=False,
    )
```

time: 976 us -> 329 us (0.34)
  waiting for transfers between devices: 878 us -> 88.5 us
  starting transfers between devices: 15.7 us -> 129 us
  local copies, waits for them, and re-layouts: 3.41 us -> 46.2 us
  other arithmetic: 5.3 us -> 22.5 us
  between operations: 14.2 us -> 1.28 us
  blocking collectives: 30.3 us -> 18.3 us
    all_gather x5 -> x0, waiting for transfers between devices: 678 us -> none  [the longest x1 158 us: per_device(): lax.all_gather(down_weight, 'gx', axis=1, tiled=True)]
    psum x1 -> x0, waiting for transfers between devices: 148 us -> none  [per_device(): gate, upper = lax.psum((gate_part, upper_part), 'gz')]
    ppermute x0 -> x20, starting transfers between devices: none -> 110 us  [the longest x14 66.6 us: shift(): return lax.ppermute(value, DEPTH, [(i, (i + by) % 16) for i in range(16)])]
    ppermute x0 -> x20, waiting for transfers between devices: none -> 77.7 us  [the longest x14 69.5 us: shift(): return lax.ppermute(value, DEPTH, [(i, (i + by) % 16) for i in range(16)])]
    all_gather x2 -> x0, blocking collectives: 30.3 us -> none  [the longest x1 18.4 us: per_device(): lax.all_gather(tokens, 'gy', axis=1, tiled=True)]
    reduce_scatter x2 -> x0, waiting for transfers between devices: 19.3 us -> none  [the longest x1 19.2 us: per_device(): lax.psum_scatter(output_part, 'gy', scatter_dimension=1, tiled=True)]
    all_to_all x3 -> x4, waiting for transfers between devices: 29.9 us -> 10.8 us  [the longest x1 10.8 us: per_device(): gate_up = lax.all_to_all(gate_up, 'x', 1, 0).reshape(4 * tok, 2 * cols)]
    all_to_all x0 -> x1, blocking collectives: none -> 18.3 us  [gather_plane(): own = lax.all_to_all(both, ('x', 'y'), 0, 0, tiled=True)]
  transfers between devices with their start and end apart: 11 -> 24, of which waited for: 9 -> 11; matrix products, arithmetic and copies ran while one was open for 2% -> 24% of each run, Pallas kernels for 0% -> 0%
where the time goes in v1:
time: 329 us; the launch traced here: 327 us
  starting transfers between devices  129 us (39%)
  waiting for transfers between devices  88.5 us (27%)
  local copies, waits for them, and re-layouts  46.2 us (14%)
  other arithmetic  22.5 us (7%)
  matrix products  20.3 us (6%)
  blocking collectives  18.3 us (6%)
    ppermute x14, waiting for transfers between devices, shift(): return lax.ppermute(value, DEPTH, [(i, (i + by) % 16) for i in range(16)])  69.5 us
    ppermute x14, starting transfers between devices, shift(): return lax.ppermute(value, DEPTH, [(i, (i + by) % 16) for i in range(16)])  66.6 us
    dot_general x15, matrix products, dot(): lax.dot_general(left, right, (((left_dim,), (right_dim,)), ((), ())), pre...  20.3 us
    ppermute x3, starting transfers between devices, swap(): return lax.ppermute(value, axis, [(0, 1), (1, 0)])  18.6 us
    all_to_all x1, blocking collectives, gather_plane(): own = lax.all_to_all(both, ('x', 'y'), 0, 0, tiled=True)  18.3 us
    ppermute x1, starting transfers between devices, per_device(): near = lax.ppermute(both, ('zh', 'c'), [(0, 0), (1, 2), (2, 1), (3, 3)])  17 us
    all_to_all x1, waiting for transfers between devices, per_device(): gate_up = lax.all_to_all(gate_up, 'x', 1, 0).reshape(4 * tok, 2 * cols)  10.8 us
    slice x2, local copies, waits for them, and re-layouts, per_device(): down_grad = dot(own_half(2 * cols), whole[1], 0, 0)  9.14 us
  transfers between devices with their start and end apart: 24, of which 11 were waited for; matrix products, arithmetic and copies ran while one was open for 24% of the time, Pallas kernels for 0%

profile of v1, /device:TPU:1, one launch (start us, length us, event | category | flops | bytes accessed | tf_op | source)
XLA Modules:
  0.0 326.6 jit_solution(5452796349517102337)
XLA Ops:
  2.1 17.0 %collective-permute-start = (bf16[2,128,128]{2,1,0:T(8,128)(2,1)}, bf16[2,128,128]{2,1,0:T(8,128)(2,1)S(1)}, u32[]{:S(2)}, u32[]{:S(2)}) collective-permute-start(bf16[2,128,128]{2,1,0:T(8,128)(2,1)} %pad_maximum_fusion.5), channel_id=1, source_target_pairs={{0,0},{8,64},{64,8},{72,72},{1,1},{9,65},{65,9},{73,73},{2,2},{10,... | collective-permute-start | bytes 196616 | tf_op jit(solution)/shard_map/ppermute | solution.py:51
  21.5 18.3 %all_to_all.49 = bf16[16,2,128,128]{3,2,1,0:T(8,128)(2,1)S(1)} all-to-all(bf16[16,2,128,128]{3,2,1,0:T(8,128)(2,1)S(1)} %broadcast_in_dim.51), channel_id=1, replica_groups=mesh['x'=4,'zh'=2,'y'=4,'c'=2,'gz'=8] {'x','y'}, dimensions={0} | all-to-all | bytes 2097152 | tf_op jit(solution)/shard_map/all_to_all | solution.py:38
  49.2 10.8 %all-to-all-done.1 = bf16[1,128,4,896]{1,3,0,2:T(8,128)(2,1)S(1)} async-done(((bf16[1,128,4,896]{1,3,0,2:T(8,128)(2,1)}), bf16[1,128,4,896]{1,3,0,2:T(8,128)(2,1)S(1)}, u32[]{:S(2)}, u32[]{:S(2)}) %all-to-all-start.1) | async-done | bytes 917536 | tf_op jit(solution)/shard_map/all_to_all | solution.py:57
  77.3 4.9 %all-to-all-start.4 = ((bf16[16,2,128,128]{3,2,1,0:T(8,128)(2,1)}), bf16[16,2,128,128]{3,2,1,0:T(8,128)(2,1)}, u32[]{:S(2)}, u32[]{:S(2)}) async-start(bf16[16,2,128,128]{3,2,1,0:T(8,128)(2,1)} %broadcast_in_dim.62), calls=%async_computation.4 | async-start | bytes 2097152 | tf_op jit(solution)/shard_map/all_to_all | solution.py:38
  89.3 10.1 %collective-permute-start.3 = (bf16[4,64,1344]{2,1,0:T(8,128)(2,1)}, bf16[4,64,1344]{2,1,0:T(8,128)(2,1)}, u32[]{:S(2)}, u32[]{:S(2)}) collective-permute-start(bf16[4,64,1344]{2,1,0:T(8,128)(2,1)} %bitcast.25), channel_id=1, source_target_pairs={{0,71},{1,0},{2,1},{3,2},{4,3},{5,4},{6,5},{7,6},{64,7},{65,64},{6... | collective-permute-start | bytes 2064392 | tf_op jit(solution)/shard_map/ppermute | solution.py:23
  120.8 7.9 %collective-permute-done.5 = bf16[2,64,1344]{2,1,0:T(8,128)(2,1)S(1)} collective-permute-done((bf16[2,64,1344]{2,1,0:T(8,128)(2,1)S(1)}, bf16[2,64,1344]{2,1,0:T(8,128)(2,1)S(1)}, u32[]{:S(2)}, u32[]{:S(2)}) %collective-permute-start.5) | collective-permute-done | bytes 344096 | tf_op jit(solution)/shard_map/ppermute | solution.py:23
  128.6 5.5 %collective-permute-done.4 = bf16[2,64,1344]{2,1,0:T(8,128)(2,1)S(1)} collective-permute-done((bf16[2,64,1344]{2,1,0:T(8,128)(2,1)S(1)}, bf16[2,64,1344]{2,1,0:T(8,128)(2,1)S(1)}, u32[]{:S(2)}, u32[]{:S(2)}) %collective-permute-start.4) | collective-permute-done | bytes 344096 | tf_op jit(solution)/shard_map/ppermute | solution.py:23
  137.8 4.7 %collective-permute-start.8 = (bf16[64,1344]{1,0:T(8,128)(2,1)}, bf16[64,1344]{1,0:T(8,128)(2,1)}, u32[]{:S(2)}, u32[]{:S(2)}) collective-permute-start(bf16[64,1344]{1,0:T(8,128)(2,1)} %get-tuple-element.24), channel_id=1, source_target_pairs={{0,68},{1,69},{2,70},{3,71},{4,0},{5,1},{6,2},{7,3},{64,4},{65,5},... | collective-permute-start | bytes 516104 | tf_op jit(solution)/shard_map/ppermute | solution.py:23
  142.5 4.5 %collective-permute-start.7 = (bf16[64,1344]{1,0:T(8,128)(2,1)}, bf16[64,1344]{1,0:T(8,128)(2,1)}, u32[]{:S(2)}, u32[]{:S(2)}) collective-permute-start(bf16[64,1344]{1,0:T(8,128)(2,1)} %get-tuple-element.25), channel_id=1, source_target_pairs={{0,4},{1,5},{2,6},{3,7},{4,64},{5,65},{6,66},{7,67},{64,68},{65,69... | collective-permute-start | bytes 516104 | tf_op jit(solution)/shard_map/ppermute | solution.py:23
  147.0 6.4 %collective-permute-start.6 = (bf16[64,1344]{1,0:T(8,128)(2,1)}, bf16[64,1344]{1,0:T(8,128)(2,1)}, u32[]{:S(2)}, u32[]{:S(2)}) collective-permute-start(bf16[64,1344]{1,0:T(8,128)(2,1)} %get-tuple-element.23), channel_id=1, source_target_pairs={{0,64},{1,65},{2,66},{3,67},{4,68},{5,69},{6,70},{7,71},{64,0},{65... | collective-permute-start | bytes 516104 | tf_op jit(solution)/shard_map/ppermute | solution.py:23
  153.5 8.2 %collective-permute-start.19 = (bf16[4,4,2,128,128]{4,3,2,1,0:T(8,128)(2,1)}, bf16[4,4,2,128,128]{4,3,2,1,0:T(8,128)(2,1)}, u32[]{:S(2)}, u32[]{:S(2)}) collective-permute-start(bf16[4,4,2,128,128]{4,3,2,1,0:T(8,128)(2,1)} %bitcast.58), channel_id=1, source_target_pairs={{0,8},{8,0},{1,9},{9,1},{2,10},{10,2},{3,11},{11,3},{4,12},{12,4},... | collective-permute-start | bytes 3145736 | tf_op jit(solution)/shard_map/ppermute | solution.py:19
  161.7 19.7 %collective-permute-done.6 = bf16[64,1344]{1,0:T(8,128)(2,1)} collective-permute-done((bf16[64,1344]{1,0:T(8,128)(2,1)}, bf16[64,1344]{1,0:T(8,128)(2,1)}, u32[]{:S(2)}, u32[]{:S(2)}) %collective-permute-start.6) | collective-permute-done | bytes 172064 | tf_op jit(solution)/shard_map/ppermute | solution.py:23
  185.1 9.7 %collective-permute-start.9 = (bf16[64,1344]{1,0:T(8,128)(2,1)}, bf16[64,1344]{1,0:T(8,128)(2,1)S(1)}, u32[]{:S(2)}, u32[]{:S(2)}) collective-permute-start(bf16[64,1344]{1,0:T(8,128)(2,1)} %concatenate.30), channel_id=1, source_target_pairs={{0,64},{1,65},{2,66},{3,67},{4,68},{5,69},{6,70},{7,71},{64,0},{65... | collective-permute-start | bytes 516104 | tf_op jit(solution)/shard_map/ppermute | solution.py:23
  196.8 7.3 %collective-permute-start.11 = (bf16[64,1344]{1,0:T(8,128)(2,1)}, bf16[64,1344]{1,0:T(8,128)(2,1)S(1)}, u32[]{:S(2)}, u32[]{:S(2)}) collective-permute-start(bf16[64,1344]{1,0:T(8,128)(2,1)} %concatenate.30), channel_id=1, source_target_pairs={{0,68},{1,69},{2,70},{3,71},{4,0},{5,1},{6,2},{7,3},{64,4},{65,5},... | collective-permute-start | bytes 516104 | tf_op jit(solution)/shard_map/ppermute | solution.py:23
  207.0 15.6 %collective-permute-done.10 = bf16[64,1344]{1,0:T(8,128)(2,1)S(1)} collective-permute-done((bf16[64,1344]{1,0:T(8,128)(2,1)}, bf16[64,1344]{1,0:T(8,128)(2,1)S(1)}, u32[]{:S(2)}, u32[]{:S(2)}) %collective-permute-start.10) | collective-permute-done | bytes 172064 | tf_op jit(solution)/shard_map/ppermute | solution.py:23
  226.0 4.6 %collective-permute-start.13 = (bf16[4,64,1344]{2,1,0:T(8,128)(2,1)S(1)}, bf16[4,64,1344]{2,1,0:T(8,128)(2,1)S(1)}, u32[]{:S(2)}, u32[]{:S(2)}) collective-permute-start(bf16[4,64,1344]{2,1,0:T(8,128)(2,1)S(1)} %bitcast_dynamic-update-slice_fusion.5), channel_id=1, source_target_pairs={{0,71},{1,0},{2,1},{3,2},{4,3},{5,4},{6,5},{7,6},{64,7},{65,64},{6... | collective-permute-start | bytes 2064392 | tf_op jit(solution)/shard_map/ppermute | solution.py:23
  233.0 5.5 %collective-permute-start.15 = (bf16[2,64,1344]{2,1,0:T(8,128)(2,1)S(1)}, bf16[2,64,1344]{2,1,0:T(8,128)(2,1)S(1)}, u32[]{:S(2)}, u32[]{:S(2)}) collective-permute-start(bf16[2,64,1344]{2,1,0:T(8,128)(2,1)S(1)} %get-tuple-element.26), channel_id=1, source_target_pairs={{0,70},{1,71},{2,0},{3,1},{4,2},{5,3},{6,4},{7,5},{64,6},{65,7},{6... | collective-permute-start | bytes 1032200 | tf_op jit(solution)/shard_map/ppermute | solution.py:23
  238.5 13.6 %collective-permute-done.12 = bf16[4,64,1344]{2,1,0:T(8,128)(2,1)S(1)} collective-permute-done((bf16[4,64,1344]{2,1,0:T(8,128)(2,1)S(1)}, bf16[4,64,1344]{2,1,0:T(8,128)(2,1)S(1)}, u32[]{:S(2)}, u32[]{:S(2)}) %collective-permute-start.12) | collective-permute-done | bytes 688160 | tf_op jit(solution)/shard_map/ppermute | solution.py:23
  260.9 8.4 %collective-permute-start.16 = (f32[2,512,512]{2,1,0:T(8,128)}, f32[2,512,512]{2,1,0:T(8,128)}, u32[]{:S(2)}, u32[]{:S(2)}) collective-permute-start(f32[2,512,512]{2,1,0:T(8,128)} %pad_maximum_fusion), channel_id=1, source_target_pairs={{0,8},{8,0},{1,9},{9,1},{2,10},{10,2},{3,11},{11,3},{4,12},{12,4},... | collective-permute-start | bytes 6291464 | tf_op jit(solution)/shard_map/ppermute | solution.py:19
  278.5 8.0 %all-to-all-start.3 = ((bf16[16,2,128,128]{3,2,1,0:T(8,128)(2,1)}), bf16[16,2,128,128]{3,2,1,0:T(8,128)(2,1)}, u32[]{:S(2)}, u32[]{:S(2)}) async-start(bf16[16,2,128,128]{3,2,1,0:T(8,128)(2,1)} %bitcast.55), calls=%async_computation.3 | async-start | bytes 2097152 | tf_op jit(solution)/shard_map/all_to_all | solution.py:126
  295.5 5.1 %copy.85 = bf16[1,4,2,128,4,2,128]{6,5,4,3,2,1,0:T(2,128)(2,1)} copy(bf16[1,4,2,128,4,2,128]{6,3,0,4,1,2,5:T(8,128)(2,1)} %get-tuple-element.5) | data formatting | bytes 4194304 | tf_op jit(solution)/shard_map/slice | solution.py:142
  300.6 4.6 %squeeze.64 = bf16[1024,1024]{1,0:T(8,128)(2,1)} reshape(bf16[1,4,2,128,4,2,128]{6,5,4,3,2,1,0:T(2,128)(2,1)} %copy.85) | data formatting | bytes 4194304 | tf_op jit(solution)/shard_map/squeeze | solution.py:142
  311.6 5.1 %collective-permute-start.17 = (bf16[2,128,128]{2,1,0:T(8,128)(2,1)S(1)}, bf16[2,128,128]{2,1,0:T(8,128)(2,1)S(1)}, u32[]{:S(2)}, u32[]{:S(2)}) collective-permute-start(bf16[2,128,128]{2,1,0:T(8,128)(2,1)S(1)} %reduce_sum.12), channel_id=1, source_target_pairs={{0,0},{8,64},{64,8},{72,72},{1,1},{9,65},{65,9},{73,73},{2,2},{10,... | collective-permute-start | bytes 196616 | tf_op jit(solution)/shard_map/ppermute | solution.py:130
  319.8 6.1 %collective-permute-done.17 = bf16[2,128,128]{2,1,0:T(8,128)(2,1)S(1)} collective-permute-done((bf16[2,128,128]{2,1,0:T(8,128)(2,1)S(1)}, bf16[2,128,128]{2,1,0:T(8,128)(2,1)S(1)}, u32[]{:S(2)}, u32[]{:S(2)}) %collective-permute-start.17) | collective-permute-done | bytes 65568 | tf_op jit(solution)/shard_map/ppermute | solution.py:130
  (115 shorter events, 113.8 us)
Async XLA Ops:
  2.1 19.1 %collective-permute-start = (bf16[2,128,128]{2,1,0:T(8,128)(2,1)}, bf16[2,128,128]{2,1,0:T(8,128)(2,1)S(1)}, u32[]{:S(2)}, u32[]{:S(2)}) collective-permute-start(bf16[2,128,128]{2,1,0:T(8,128)(2,1)} %pad_maximum_fusion.5), channel_id=1, source_target_pairs={{0,0},{8,64},{64,8},{72,72},{1,1},{9,65},{65,9},{73,73},{2,2},{10,... | collective-permute-start | bytes 196616 | tf_op jit(solution)/shard_map/ppermute | solution.py:51
  39.8 24.3 %collective-permute-start.1 = (bf16[4,4,2,128,128]{4,3,2,1,0:T(8,128)(2,1)S(1)}, bf16[4,4,2,128,128]{4,3,2,1,0:T(8,128)(2,1)}, u32[]{:S(2)}, u32[]{:S(2)}) collective-permute-start(bf16[4,4,2,128,128]{4,3,2,1,0:T(8,128)(2,1)S(1)} %bitcast.169), channel_id=1, source_target_pairs={{0,8},{8,0},{1,9},{9,1},{2,10},{10,2},{3,11},{11,3},{4,12},{12,4},... | collective-permute-start | bytes 3145736 | tf_op jit(solution)/shard_map/ppermute | solution.py:19
  43.2 16.8 %all-to-all-start.1 = ((bf16[1,128,4,896]{1,3,0,2:T(8,128)(2,1)}), bf16[1,128,4,896]{1,3,0,2:T(8,128)(2,1)S(1)}, u32[]{:S(2)}, u32[]{:S(2)}) async-start(bf16[1,128,4,896]{1,3,0,2:T(8,128)(2,1)} %maximum_bitcast_fusion.3), calls=%async_computation.1 | async-start | bytes 1835008 | tf_op jit(solution)/shard_map/all_to_all | solution.py:57
  46.7 29.3 %collective-permute-start.18 = (bf16[2,128,128]{2,1,0:T(8,128)(2,1)}, bf16[2,128,128]{2,1,0:T(8,128)(2,1)S(1)}, u32[]{:S(2)}, u32[]{:S(2)}) collective-permute-start(bf16[2,128,128]{2,1,0:T(8,128)(2,1)} %pad_maximum_fusion.5), channel_id=1, source_target_pairs={{0,64},{8,0},{64,72},{72,8},{1,65},{9,1},{65,73},{73,9},{2,66},{10... | collective-permute-start | bytes 196616 | tf_op jit(solution)/shard_map/ppermute | solution.py:52
  60.0 16.1 %all-to-all-start.2 = ((bf16[4,448,128]{2,1,0:T(8,128)(2,1)}), bf16[4,448,128]{2,1,0:T(8,128)(2,1)S(1)}, u32[]{:S(2)}, u32[]{:S(2)}) async-start(bf16[4,448,128]{2,1,0:T(8,128)(2,1)} %bitcast.182), calls=%async_computation.2 | async-start | bytes 917504 | tf_op jit(solution)/shard_map/all_to_all | solution.py:58
  77.3 76.2 %all-to-all-start.4 = ((bf16[16,2,128,128]{3,2,1,0:T(8,128)(2,1)}), bf16[16,2,128,128]{3,2,1,0:T(8,128)(2,1)}, u32[]{:S(2)}, u32[]{:S(2)}) async-start(bf16[16,2,128,128]{3,2,1,0:T(8,128)(2,1)} %broadcast_in_dim.62), calls=%async_computation.4 | async-start | bytes 2097152 | tf_op jit(solution)/shard_map/all_to_all | solution.py:38
  89.3 44.9 %collective-permute-start.3 = (bf16[4,64,1344]{2,1,0:T(8,128)(2,1)}, bf16[4,64,1344]{2,1,0:T(8,128)(2,1)}, u32[]{:S(2)}, u32[]{:S(2)}) collective-permute-start(bf16[4,64,1344]{2,1,0:T(8,128)(2,1)} %bitcast.25), channel_id=1, source_target_pairs={{0,71},{1,0},{2,1},{3,2},{4,3},{5,4},{6,5},{7,6},{64,7},{65,64},{6... | collective-permute-start | bytes 2064392 | tf_op jit(solution)/shard_map/ppermute | solution.py:23
  105.5 28.7 %collective-permute-start.2 = (bf16[4,64,1344]{2,1,0:T(8,128)(2,1)}, bf16[4,64,1344]{2,1,0:T(8,128)(2,1)}, u32[]{:S(2)}, u32[]{:S(2)}) collective-permute-start(bf16[4,64,1344]{2,1,0:T(8,128)(2,1)} %bitcast.22), channel_id=1, source_target_pairs={{0,1},{1,2},{2,3},{3,4},{4,5},{5,6},{6,7},{7,64},{64,65},{65,66},{... | collective-permute-start | bytes 2064392 | tf_op jit(solution)/shard_map/ppermute | solution.py:23
  112.7 15.9 %collective-permute-start.5 = (bf16[2,64,1344]{2,1,0:T(8,128)(2,1)S(1)}, bf16[2,64,1344]{2,1,0:T(8,128)(2,1)S(1)}, u32[]{:S(2)}, u32[]{:S(2)}) collective-permute-start(bf16[2,64,1344]{2,1,0:T(8,128)(2,1)S(1)} %bitcast.184), channel_id=1, source_target_pairs={{0,70},{1,71},{2,0},{3,1},{4,2},{5,3},{6,4},{7,5},{64,6},{65,7},{6... | collective-permute-start | bytes 1032200 | tf_op jit(solution)/shard_map/ppermute | solution.py:23
  116.5 17.7 %collective-permute-start.4 = (bf16[2,64,1344]{2,1,0:T(8,128)(2,1)S(1)}, bf16[2,64,1344]{2,1,0:T(8,128)(2,1)S(1)}, u32[]{:S(2)}, u32[]{:S(2)}) collective-permute-start(bf16[2,64,1344]{2,1,0:T(8,128)(2,1)S(1)} %bitcast.183), channel_id=1, source_target_pairs={{0,2},{1,3},{2,4},{3,5},{4,6},{5,7},{6,64},{7,65},{64,66},{65,67},... | collective-permute-start | bytes 1032200 | tf_op jit(solution)/shard_map/ppermute | solution.py:23
  137.8 23.9 %collective-permute-start.8 = (bf16[64,1344]{1,0:T(8,128)(2,1)}, bf16[64,1344]{1,0:T(8,128)(2,1)}, u32[]{:S(2)}, u32[]{:S(2)}) collective-permute-start(bf16[64,1344]{1,0:T(8,128)(2,1)} %get-tuple-element.24), channel_id=1, source_target_pairs={{0,68},{1,69},{2,70},{3,71},{4,0},{5,1},{6,2},{7,3},{64,4},{65,5},... | collective-permute-start | bytes 516104 | tf_op jit(solution)/shard_map/ppermute | solution.py:23
  142.5 19.2 %collective-permute-start.7 = (bf16[64,1344]{1,0:T(8,128)(2,1)}, bf16[64,1344]{1,0:T(8,128)(2,1)}, u32[]{:S(2)}, u32[]{:S(2)}) collective-permute-start(bf16[64,1344]{1,0:T(8,128)(2,1)} %get-tuple-element.25), channel_id=1, source_target_pairs={{0,4},{1,5},{2,6},{3,7},{4,64},{5,65},{6,66},{7,67},{64,68},{65,69... | collective-permute-start | bytes 516104 | tf_op jit(solution)/shard_map/ppermute | solution.py:23
  147.0 34.4 %collective-permute-start.6 = (bf16[64,1344]{1,0:T(8,128)(2,1)}, bf16[64,1344]{1,0:T(8,128)(2,1)}, u32[]{:S(2)}, u32[]{:S(2)}) collective-permute-start(bf16[64,1344]{1,0:T(8,128)(2,1)} %get-tuple-element.23), channel_id=1, source_target_pairs={{0,64},{1,65},{2,66},{3,67},{4,68},{5,69},{6,70},{7,71},{64,0},{65... | collective-permute-start | bytes 516104 | tf_op jit(solution)/shard_map/ppermute | solution.py:23
  153.5 115.9 %collective-permute-start.19 = (bf16[4,4,2,128,128]{4,3,2,1,0:T(8,128)(2,1)}, bf16[4,4,2,128,128]{4,3,2,1,0:T(8,128)(2,1)}, u32[]{:S(2)}, u32[]{:S(2)}) collective-permute-start(bf16[4,4,2,128,128]{4,3,2,1,0:T(8,128)(2,1)} %bitcast.58), channel_id=1, source_target_pairs={{0,8},{8,0},{1,9},{9,1},{2,10},{10,2},{3,11},{11,3},{4,12},{12,4},... | collective-permute-start | bytes 3145736 | tf_op jit(solution)/shard_map/ppermute | solution.py:19
  185.1 21.9 %collective-permute-start.9 = (bf16[64,1344]{1,0:T(8,128)(2,1)}, bf16[64,1344]{1,0:T(8,128)(2,1)S(1)}, u32[]{:S(2)}, u32[]{:S(2)}) collective-permute-start(bf16[64,1344]{1,0:T(8,128)(2,1)} %concatenate.30), channel_id=1, source_target_pairs={{0,64},{1,65},{2,66},{3,67},{4,68},{5,69},{6,70},{7,71},{64,0},{65... | collective-permute-start | bytes 516104 | tf_op jit(solution)/shard_map/ppermute | solution.py:23
  194.8 27.8 %collective-permute-start.10 = (bf16[64,1344]{1,0:T(8,128)(2,1)}, bf16[64,1344]{1,0:T(8,128)(2,1)S(1)}, u32[]{:S(2)}, u32[]{:S(2)}) collective-permute-start(bf16[64,1344]{1,0:T(8,128)(2,1)} %concatenate.30), channel_id=1, source_target_pairs={{0,4},{1,5},{2,6},{3,7},{4,64},{5,65},{6,66},{7,67},{64,68},{65,69... | collective-permute-start | bytes 516104 | tf_op jit(solution)/shard_map/ppermute | solution.py:23
  196.8 27.3 %collective-permute-start.11 = (bf16[64,1344]{1,0:T(8,128)(2,1)}, bf16[64,1344]{1,0:T(8,128)(2,1)S(1)}, u32[]{:S(2)}, u32[]{:S(2)}) collective-permute-start(bf16[64,1344]{1,0:T(8,128)(2,1)} %concatenate.30), channel_id=1, source_target_pairs={{0,68},{1,69},{2,70},{3,71},{4,0},{5,1},{6,2},{7,3},{64,4},{65,5},... | collective-permute-start | bytes 516104 | tf_op jit(solution)/shard_map/ppermute | solution.py:23
  224.1 28.0 %collective-permute-start.12 = (bf16[4,64,1344]{2,1,0:T(8,128)(2,1)S(1)}, bf16[4,64,1344]{2,1,0:T(8,128)(2,1)S(1)}, u32[]{:S(2)}, u32[]{:S(2)}) collective-permute-start(bf16[4,64,1344]{2,1,0:T(8,128)(2,1)S(1)} %bitcast_dynamic-update-slice_fusion.5), channel_id=1, source_target_pairs={{0,1},{1,2},{2,3},{3,4},{4,5},{5,6},{6,7},{7,64},{64,65},{65,66},{... | collective-permute-start | bytes 2064392 | tf_op jit(solution)/shard_map/ppermute | solution.py:23
  226.0 26.2 %collective-permute-start.13 = (bf16[4,64,1344]{2,1,0:T(8,128)(2,1)S(1)}, bf16[4,64,1344]{2,1,0:T(8,128)(2,1)S(1)}, u32[]{:S(2)}, u32[]{:S(2)}) collective-permute-start(bf16[4,64,1344]{2,1,0:T(8,128)(2,1)S(1)} %bitcast_dynamic-update-slice_fusion.5), channel_id=1, source_target_pairs={{0,71},{1,0},{2,1},{3,2},{4,3},{5,4},{6,5},{7,6},{64,7},{65,64},{6... | collective-permute-start | bytes 2064392 | tf_op jit(solution)/shard_map/ppermute | solution.py:23
  231.1 21.2 %collective-permute-start.14 = (bf16[2,64,1344]{2,1,0:T(8,128)(2,1)S(1)}, bf16[2,64,1344]{2,1,0:T(8,128)(2,1)S(1)}, u32[]{:S(2)}, u32[]{:S(2)}) collective-permute-start(bf16[2,64,1344]{2,1,0:T(8,128)(2,1)S(1)} %get-tuple-element.27), channel_id=1, source_target_pairs={{0,2},{1,3},{2,4},{3,5},{4,6},{5,7},{6,64},{7,65},{64,66},{65,67},... | collective-permute-start | bytes 1032200 | tf_op jit(solution)/shard_map/ppermute | solution.py:23
  233.0 23.0 %collective-permute-start.15 = (bf16[2,64,1344]{2,1,0:T(8,128)(2,1)S(1)}, bf16[2,64,1344]{2,1,0:T(8,128)(2,1)S(1)}, u32[]{:S(2)}, u32[]{:S(2)}) collective-permute-start(bf16[2,64,1344]{2,1,0:T(8,128)(2,1)S(1)} %get-tuple-element.26), channel_id=1, source_target_pairs={{0,70},{1,71},{2,0},{3,1},{4,2},{5,3},{6,4},{7,5},{64,6},{65,7},{6... | collective-permute-start | bytes 1032200 | tf_op jit(solution)/shard_map/ppermute | solution.py:23
  260.9 14.2 %collective-permute-start.16 = (f32[2,512,512]{2,1,0:T(8,128)}, f32[2,512,512]{2,1,0:T(8,128)}, u32[]{:S(2)}, u32[]{:S(2)}) collective-permute-start(f32[2,512,512]{2,1,0:T(8,128)} %pad_maximum_fusion), channel_id=1, source_target_pairs={{0,8},{8,0},{1,9},{9,1},{2,10},{10,2},{3,11},{11,3},{4,12},{12,4},... | collective-permute-start | bytes 6291464 | tf_op jit(solution)/shard_map/ppermute | solution.py:19
  278.5 31.7 %all-to-all-start.3 = ((bf16[16,2,128,128]{3,2,1,0:T(8,128)(2,1)}), bf16[16,2,128,128]{3,2,1,0:T(8,128)(2,1)}, u32[]{:S(2)}, u32[]{:S(2)}) async-start(bf16[16,2,128,128]{3,2,1,0:T(8,128)(2,1)} %bitcast.55), calls=%async_computation.3 | async-start | bytes 2097152 | tf_op jit(solution)/shard_map/all_to_all | solution.py:126
  311.6 14.3 %collective-permute-start.17 = (bf16[2,128,128]{2,1,0:T(8,128)(2,1)S(1)}, bf16[2,128,128]{2,1,0:T(8,128)(2,1)S(1)}, u32[]{:S(2)}, u32[]{:S(2)}) collective-permute-start(bf16[2,128,128]{2,1,0:T(8,128)(2,1)S(1)} %reduce_sum.12), channel_id=1, source_target_pairs={{0,0},{8,64},{64,8},{72,72},{1,1},{9,65},{65,9},{73,73},{2,2},{10,... | collective-permute-start | bytes 196616 | tf_op jit(solution)/shard_map/ppermute | solution.py:130
  (12 other events, 131.9 us)

commit v2 on v1

v2 whole, which is shorter than its diff:
```python
import jax
import jax.numpy as jnp
from jax import lax
from jax.experimental import pallas as pl
from jax.experimental.pallas import tpu as pltpu
from jax.sharding import Mesh, PartitionSpec as P

BF = jnp.bfloat16
F32 = jnp.float32
DEPTH = ("zh", "gz")
TURN = [(0, 0), (1, 2), (2, 1), (3, 3)]


def dot(left, right, left_dim, right_dim):
    return lax.dot_general(
        left, right, (((left_dim,), (right_dim,)), ((), ())), preferred_element_type=F32
    )


def swap(value, axis):
    return lax.ppermute(value, axis, [(0, 1), (1, 0)])


def take(value, index, dim=0):
    return lax.dynamic_index_in_dim(value, index, dim, keepdims=False)


def tokens_of(ref, array, ys):
    return jnp.concatenate(
        [jnp.concatenate([ref[x, y, array] for x in range(4)], axis=0) for y in ys],
        axis=1,
    )


def partial_kernel(core_ref, own_ref, other_ref, weight_ref, out_ref):
    cols = weight_ref.shape[2] // 3
    tok = own_ref.shape[3]
    weight = weight_ref[...].reshape(-1, 3 * cols)

    def work(ref, k):
        pair = dot(tokens_of(ref, 0, range(4)), weight[:, : 2 * cols], 1, 0)
        last = dot(tokens_of(ref, 1, range(4)), weight[:, 2 * cols :], 1, 0)
        out_ref[:, k, :, : 2 * cols] = pair.reshape(4, tok, 2 * cols)
        out_ref[:, k, :, 2 * cols :] = last.reshape(4, tok, cols)

    for core in range(2):

        @pl.when(core_ref[0] == core)
        def _():
            work(own_ref, core)
            work(other_ref, 1 - core)


def parts_kernel(which_ref, rows_ref, weight_ref, *rest):
    cols = weight_ref.shape[2] // 3
    rows = rows_ref[:, which_ref[0]].reshape(-1, 3 * cols)
    weight = weight_ref[...].reshape(-1, 3 * cols)
    output = dot(rows[:, 2 * cols :], weight[:, 2 * cols :], 1, 1)
    inner = dot(rows[:, : 2 * cols], weight[:, : 2 * cols], 1, 1)
    if len(rest) == 1:
        rest[0][0] = output
        rest[0][1] = inner
        return
    got_ref, out_ref = rest
    tok, feat = out_ref.shape[3:]
    for index, value in enumerate((output, inner)):
        value = (value + got_ref[index]).astype(BF)
        for x in range(4):
            for y in range(4):
                out_ref[x, y, index] = value[
                    x * tok : (x + 1) * tok, y * feat : (y + 1) * feat
                ]


def grads_kernel(place_ref, pieces_ref, rows_ref, gate_ref, up_ref, down_ref):
    part = gate_ref.shape[0]
    zh, core = place_ref[0], place_ref[1]
    width = 2 * pieces_ref.shape[6]
    for y in range(4):
        blocks = []
        for array in range(2):
            sides = []
            for parity in range(2):
                far = jnp.where(zh == parity, 0, 1)
                rows = []
                for x in range(4):
                    for k in range(2):
                        other = jnp.where(core == k, 0, 1)
                        rows.append(pieces_ref[far, other, x, y, array])
                sides.append(jnp.concatenate(rows, axis=0))
            blocks.append(jnp.concatenate(sides, axis=1))
        at = slice(y * width, (y + 1) * width)
        pair = dot(rows_ref[: 2 * part], blocks[0], 1, 0).astype(BF)
        gate_ref[:, at] = pair[:part]
        up_ref[:, at] = pair[part:]
        down_ref[:, at] = dot(rows_ref[2 * part :], blocks[1], 1, 0).astype(BF)


def local_call(kernel, shape, flops, scalars, *arrays):
    smem = pl.BlockSpec(memory_space=pltpu.SMEM)
    vmem = pl.BlockSpec(memory_space=pltpu.VMEM)
    return pl.pallas_call(
        kernel,
        out_shape=shape,
        in_specs=[smem] + [vmem] * len(arrays),
        out_specs=jax.tree.map(lambda _: vmem, shape),
        compiler_params=pltpu.CompilerParams(vmem_limit_bytes=40 * 2**20),
        cost_estimate=pl.CostEstimate(
            flops=flops, bytes_accessed=6 * 2**20, transcendentals=0
        ),
    )(scalars, *arrays)


def gather_plane(both):
    both = jnp.broadcast_to(both[None], (16,) + both.shape)
    own = lax.all_to_all(both, ("x", "y"), 0, 0, tiled=True)
    own = own.reshape((4, 4) + own.shape[1:])
    return own, swap(own, "c")


def per_device(tokens, cotangent, gate_weight, up_weight, down_weight):
    x, zh, core = (lax.axis_index(name) for name in ("x", "zh", "c"))
    tok, feat = tokens.shape
    cols = gate_weight.shape[1] // 4
    wide = 3 * cols
    flops = 2 * 8 * tok * 4 * feat * wide

    both = jnp.stack([tokens, cotangent])
    near = lax.ppermute(both, ("zh", "c"), TURN)

    mixed = jnp.concatenate(
        [
            gate_weight.reshape(tok, 4, cols),
            up_weight.reshape(tok, 4, cols),
            down_weight.T.reshape(tok, 4, cols),
        ],
        axis=2,
    ).transpose(1, 0, 2)
    weight = jnp.zeros_like(mixed)
    weight = lax.dynamic_update_index_in_dim(weight, take(mixed, x), x, 0)
    for by in (1, 2, 3):
        sent = lax.ppermute(
            take(mixed, lax.rem(x + by, 4)), "x", [(i, (i + by) % 4) for i in range(4)]
        )
        weight = lax.dynamic_update_index_in_dim(weight, sent, lax.rem(x + 4 - by, 4), 0)

    own, other = gather_plane(near)

    part = local_call(
        partial_kernel,
        jax.ShapeDtypeStruct((4, 2, tok, wide), F32),
        flops,
        jnp.stack([core]),
        own,
        other,
        weight,
    )
    both, part = lax.optimization_barrier((both, part))
    total = lax.psum_scatter(
        part.reshape(8 * tok, wide), DEPTH, scatter_dimension=0, tiled=True
    )

    far = lax.ppermute(both, ("zh", "c"), [(0, 2), (1, 0), (2, 3), (3, 1)])
    far_own, far_other = gather_plane(far)
    pieces = jnp.stack([own, other, far_own, far_other])
    pieces = pieces.reshape((2, 2) + own.shape)

    gate, upper, hidden_grad = (total[:, i * cols : (i + 1) * cols] for i in range(3))
    sigma = jax.nn.sigmoid(gate)
    activated = gate * sigma
    hidden = (activated * upper).astype(BF)
    gate_delta = (hidden_grad * upper * sigma * (1.0 + gate * (1.0 - sigma))).astype(BF)
    up_delta = (hidden_grad * activated).astype(BF)
    mine = jnp.concatenate([gate_delta, up_delta, hidden], axis=1)
    mine, pieces = lax.optimization_barrier((mine, pieces))
    every = lax.all_gather(mine, DEPTH, axis=0, tiled=True)

    by_zh = every.reshape(4, 2, tok, wide)
    give = local_call(
        parts_kernel,
        jax.ShapeDtypeStruct((2, 4 * tok, 4 * feat), F32),
        flops // 2,
        jnp.stack([1 - core]),
        by_zh,
        weight,
    )
    sums = local_call(
        parts_kernel,
        jax.ShapeDtypeStruct((4, 4, 2, tok, feat), BF),
        flops // 2,
        jnp.stack([core]),
        by_zh,
        weight,
        swap(give, "c"),
    )
    sums = lax.all_to_all(
        sums.reshape(16, 2, tok, feat), ("x", "y"), 0, 0, tiled=True
    )
    result = jnp.sum(sums.astype(F32), axis=0).astype(BF)
    result = lax.ppermute(result, ("zh", "c"), TURN)

    half = cols // 2

    def own_half(at):
        return jnp.where(
            zh == 0, every[:, at : at + half], every[:, at + half : at + cols]
        )

    rows = jnp.concatenate([own_half(i * cols) for i in range(3)], axis=1).T
    grad = jax.ShapeDtypeStruct((half, 8 * feat), BF)
    gate_grad, up_grad, down_grad = local_call(
        grads_kernel,
        (grad, grad, grad),
        flops,
        jnp.stack([zh, core]),
        pieces,
        rows,
    )
    return result[0], result[1], gate_grad.T, up_grad.T, down_grad


def solution(mesh):
    fine = Mesh(mesh.devices.reshape(4, 2, 4, 2, 8), ("x", "zh", "y", "c", "gz"))
    gx, gy = ("x", "zh"), ("y", "c")
    act = P(gx, ("gz",) + gy)
    return jax.shard_map(
        per_device,
        mesh=fine,
        in_specs=(act, act, P(("gz",) + gx, gy), P(("gz",) + gx, gy), P(gy, ("gz",) + gx)),
        out_specs=(act, act, P("gz", gy + gx), P("gz", gy + gx), P(gy + gx, "gz")),
        check_vma=False,
    )
```

time: 329 us -> 289 us (0.88)
  starting transfers between devices: 129 us -> 72.9 us
  waiting for transfers between devices: 88.5 us -> 132 us
  matrix products: 20.3 us -> 0 us
  other arithmetic: 22.5 us -> 6.05 us
  local copies, waits for them, and re-layouts: 46.2 us -> 30.7 us
  between operations: 1.28 us -> 14.4 us
  Pallas kernels: 0 us -> 10.1 us
    ppermute x16 -> x5, waiting for transfers between devices: 77.7 us -> 1.92 us  [the longest x3 1.92 us: per_device(): lax.ppermute(take(mixed, lax.rem(x + by, 4)), 'x', [(i, (i + by) % 4) for...]
    all_gather x0 -> x1, waiting for transfers between devices: none -> 73.7 us  [per_device(): every = lax.all_gather(mine, DEPTH, axis=0, tiled=True)]
    ppermute x16 -> x5, starting transfers between devices: 88.6 us -> 39 us  [the longest x1 16.8 us: per_device(): near = lax.ppermute(both, ('zh', 'c'), TURN)]
    reduce_scatter x0 -> x1, waiting for transfers between devices: none -> 31.9 us  [per_device(): lax.psum_scatter(part.reshape(8 * tok, wide), DEPTH, scatter_dimension=0,...]
    dot_general x15 -> x0, matrix products: 20.3 us -> none  [dot(): lax.dot_general(left, right, (((left_dim,), (right_dim,)), ((), ())), pre...]
    unnamed x26 -> x38, local copies, waits for them, and re-layouts: 2.15 us -> 19.1 us
    ppermute x1, waiting for transfers between devices: 0.01 us -> 11.9 us  [per_device(): far = lax.ppermute(both, ('zh', 'c'), [(0, 2), (1, 0), (2, 3), (3, 1)])]
    slice x5 -> x1, local copies, waits for them, and re-layouts: 14.2 us -> 2.56 us  [own_half(): every[:, at + half:at + cols]]
  transfers between devices with their start and end apart: 24 -> 13, of which waited for: 11 -> 7; matrix products, arithmetic and copies ran while one was open for 24% -> 7% of each run, Pallas kernels for 0% -> 1%
where the time goes in v2:
time: 289 us; the launch traced here: 288 us
  waiting for transfers between devices  132 us (46%)
  starting transfers between devices  72.9 us (25%)
  local copies, waits for them, and re-layouts  30.7 us (11%)
  blocking collectives  21.5 us (7%)
  between operations  14.4 us (5%)
  Pallas kernels  10.1 us (3%)
  other arithmetic  6.05 us (2%)
    all_gather x1, waiting for transfers between devices, per_device(): every = lax.all_gather(mine, DEPTH, axis=0, tiled=True)  73.7 us
    reduce_scatter x1, waiting for transfers between devices, per_device(): lax.psum_scatter(part.reshape(8 * tok, wide), DEPTH, scatter_dimension=0,...  31.9 us
    all_to_all x1, blocking collectives, gather_plane(): own = lax.all_to_all(both, ('x', 'y'), 0, 0, tiled=True)  21.5 us
    unnamed x38, local copies, waits for them, and re-layouts  19.1 us
    ppermute x3, starting transfers between devices, swap(): return lax.ppermute(value, axis, [(0, 1), (1, 0)])  18.6 us
    ppermute x1, starting transfers between devices, per_device(): near = lax.ppermute(both, ('zh', 'c'), TURN)  16.8 us
    ppermute x1, waiting for transfers between devices, per_device(): far = lax.ppermute(both, ('zh', 'c'), [(0, 2), (1, 0), (2, 3), (3, 1)])  11.9 us
    ppermute x1, starting transfers between devices, per_device(): result = lax.ppermute(result, ('zh', 'c'), TURN)  11.5 us
  transfers between devices with their start and end apart: 13, of which 7 were waited for; matrix products, arithmetic and copies ran while one was open for 7% of the time, Pallas kernels for 1%

profile of v2, /device:TPU:1, one launch (start us, length us, event | category | flops | bytes accessed | tf_op | source)
XLA Modules:
  0.0 288.1 jit_solution(14513052739384661197)
XLA Ops:
  8.0 16.8 %collective-permute-start = (bf16[2,128,128]{2,1,0:T(8,128)(2,1)S(1)}, bf16[2,128,128]{2,1,0:T(8,128)(2,1)S(1)}, u32[]{:S(2)}, u32[]{:S(2)}) collective-permute-start(bf16[2,128,128]{2,1,0:T(8,128)(2,1)S(1)} %pad_maximum_fusion.2), channel_id=1, source_target_pairs={{0,0},{8,64},{64,8},{72,72},{1,1},{9,65},{65,9},{73,73},{2,2},{10,... | collective-permute-start | bytes 196616 | tf_op jit(solution)/shard_map/ppermute | solution.py:129
  28.6 6.8 %all-to-all-start = ((bf16[16,2,128,128]{3,2,1,0:T(8,128)(2,1)}), bf16[16,2,128,128]{3,2,1,0:T(8,128)(2,1)S(1)}, u32[]{:S(2)}, u32[]{:S(2)}) async-start(bf16[16,2,128,128]{3,2,1,0:T(8,128)(2,1)} %broadcast_in_dim.26), calls=%async_computation | async-start | bytes 2097152 | tf_op jit(solution)/shard_map/all_to_all | solution.py:116
  36.6 3.3 %collective-permute-start.2 = (bf16[128,1344]{1,0:T(8,128)(2,1)}, bf16[128,1344]{1,0:T(8,128)(2,1)}, u32[]{:S(2)}, u32[]{:S(2)}) collective-permute-start(bf16[128,1344]{1,0:T(8,128)(2,1)} %bitcast.10), channel_id=1, source_target_pairs={{0,128},{128,256},{256,384},{384,0},{1,129},{129,257},{257,385},{3... | collective-permute-start | bytes 1032200 | tf_op jit(solution)/shard_map/ppermute | solution.py:142
  40.8 4.3 %collective-permute-start.3 = (bf16[128,1344]{1,0:T(8,128)(2,1)}, bf16[128,1344]{1,0:T(8,128)(2,1)}, u32[]{:S(2)}, u32[]{:S(2)}) collective-permute-start(bf16[128,1344]{1,0:T(8,128)(2,1)} %bitcast.12), channel_id=1, source_target_pairs={{0,256},{128,384},{256,0},{384,128},{1,257},{129,385},{257,1},{385... | collective-permute-start | bytes 1032200 | tf_op jit(solution)/shard_map/ppermute | solution.py:142
  46.0 3.1 %collective-permute-start.4 = (bf16[128,1344]{1,0:T(8,128)(2,1)}, bf16[128,1344]{1,0:T(8,128)(2,1)}, u32[]{:S(2)}, u32[]{:S(2)}) collective-permute-start(bf16[128,1344]{1,0:T(8,128)(2,1)} %bitcast.14), channel_id=1, source_target_pairs={{0,384},{128,0},{256,128},{384,256},{1,385},{129,1},{257,129},{385... | collective-permute-start | bytes 1032200 | tf_op jit(solution)/shard_map/ppermute | solution.py:142
  49.4 1.9 collective-permute-start.1
  58.3 2.5 copy-done.2
  63.6 11.9 %collective-permute-done.5 = bf16[2,128,128]{2,1,0:T(8,128)(2,1)S(1)} collective-permute-done((bf16[2,128,128]{2,1,0:T(8,128)(2,1)S(1)}, bf16[2,128,128]{2,1,0:T(8,128)(2,1)S(1)}, u32[]{:S(2)}, u32[]{:S(2)}) %collective-permute-start.5) | collective-permute-done | bytes 65568 | tf_op jit(solution)/shard_map/ppermute | solution.py:163
  75.7 21.5 %all_to_all.15 = bf16[16,2,128,128]{3,2,1,0:T(8,128)(2,1)S(1)} all-to-all(bf16[16,2,128,128]{3,2,1,0:T(8,128)(2,1)S(1)} %broadcast_in_dim.31), channel_id=1, replica_groups=mesh['x'=4,'zh'=2,'y'=4,'c'=2,'gz'=8] {'x','y'}, dimensions={0} | all-to-all | bytes 2097152 | tf_op jit(solution)/shard_map/all_to_all | solution.py:116
  97.2 5.1 %collective-permute-start.6 = (bf16[4,4,2,128,128]{4,3,2,1,0:T(8,128)(2,1)S(1)}, bf16[4,4,2,128,128]{4,3,2,1,0:T(8,128)(2,1)S(1)}, u32[]{:S(2)}, u32[]{:S(2)}) collective-permute-start(bf16[4,4,2,128,128]{4,3,2,1,0:T(8,128)(2,1)S(1)} %bitcast.49), channel_id=1, source_target_pairs={{0,8},{8,0},{1,9},{9,1},{2,10},{10,2},{3,11},{11,3},{4,12},{12,4},... | collective-permute-start | bytes 3145736 | tf_op jit(solution)/shard_map/ppermute | solution.py:21
  102.3 2.3 collective-permute-done.6
  104.6 2.3 pad_maximum_fusion
  106.9 31.9 %reduce-scatter.4.cloned.1.call-done = f32[64,1344]{1,0:T(8,128)} async-done(((f32[1024,1344]{1,0:T(8,128)}), f32[64,1344]{1,0:T(8,128)}) %reduce-scatter.4.cloned.1.call-update) | async-done | bytes 344080 | tf_op jit(solution)/shard_map/reduce_scatter | solution.py:159
  140.7 73.7 %all-gather.2.cloned.1.call-done = bf16[1024,1344]{1,0:T(8,128)(2,1)} async-done(((bf16[64,1344]{1,0:T(8,128)(2,1)}), bf16[1024,1344]{1,0:T(8,128)(2,1)}) %all-gather.2.cloned.1.call-update) | async-done | bytes 2752528 | tf_op jit(solution)/shard_map/all_gather | solution.py:176
  217.6 2.4 shard_map.93
  220.0 11.6 %collective-permute-start.7 = (f32[2,512,512]{2,1,0:T(8,128)}, f32[2,512,512]{2,1,0:T(8,128)}, u32[]{:S(2)}, u32[]{:S(2)}) collective-permute-start(f32[2,512,512]{2,1,0:T(8,128)} %shard_map.93), channel_id=1, source_target_pairs={{0,8},{8,0},{1,9},{9,1},{2,10},{10,2},{3,11},{11,3},{4,12},{12,4},... | collective-permute-start | bytes 6291464 | tf_op jit(solution)/shard_map/ppermute | solution.py:21
  231.7 4.0 %collective-permute-done.7.rest_0_ = f32[2,512,512]{2,1,0:T(8,128)} collective-permute-done((f32[2,512,512]{2,1,0:T(8,128)}, f32[2,512,512]{2,1,0:T(8,128)}, u32[]{:S(2)}, u32[]{:S(2)}) %collective-permute-start.7) | collective-permute-done | bytes 2097184 | tf_op jit(solution)/shard_map/ppermute | solution.py:21
  237.1 2.6 shard_map.94
  240.7 6.6 %all-to-all-start.2 = ((bf16[16,2,128,128]{3,2,1,0:T(8,128)(2,1)}), bf16[16,2,128,128]{3,2,1,0:T(8,128)(2,1)}, u32[]{:S(2)}, u32[]{:S(2)}) async-start(bf16[16,2,128,128]{3,2,1,0:T(8,128)(2,1)} %bitcast.48), calls=%async_computation.2 | async-start | bytes 2097152 | tf_op jit(solution)/shard_map/all_to_all | solution.py:196
  247.3 2.6 fusion.1
  255.7 6.7 %all-to-all-done.2 = bf16[16,2,128,128]{3,2,1,0:T(8,128)(2,1)} async-done(((bf16[16,2,128,128]{3,2,1,0:T(8,128)(2,1)}), bf16[16,2,128,128]{3,2,1,0:T(8,128)(2,1)}, u32[]{:S(2)}, u32[]{:S(2)}) %all-to-all-start.2) | async-done | bytes 1048608 | tf_op jit(solution)/shard_map/all_to_all | solution.py:196
  263.8 11.5 %collective-permute-start.8 = (bf16[2,128,128]{2,1,0:T(8,128)(2,1)S(1)}, bf16[2,128,128]{2,1,0:T(8,128)(2,1)S(1)}, u32[]{:S(2)}, u32[]{:S(2)}) collective-permute-start(bf16[2,128,128]{2,1,0:T(8,128)(2,1)S(1)} %reduce_sum.12), channel_id=1, source_target_pairs={{0,0},{8,64},{64,8},{72,72},{1,1},{9,65},{65,9},{73,73},{2,2},{10,... | collective-permute-start | bytes 196616 | tf_op jit(solution)/shard_map/ppermute | solution.py:200
  275.3 2.2 copy-done.6
  277.5 3.2 %shard_map.95 = (bf16[224,1024]{1,0:T(8,128)(2,1)}, bf16[224,1024]{1,0:T(8,128)(2,1)}, bf16[224,1024]{1,0:T(8,128)(2,1)}) custom-call(s32[2]{0:T(128)S(1)} %pad_add_fusion.place_ref, bf16[2,2,4,4,2,128,128]{6,5,4,3,2,1,0:T(8,128)(2,1)S(1)} %bitcast.43, bf16[672,1024]{1,0:T(8,128)(2,1)S(1)} %maximum_bitcast_fusion.rows_ref), custom_call_target="tpu_custom_call" | custom-call | flops 1409286144 | bytes 6291456 | tf_op jit(solution)/shard_map/pallas_call | solution.py:102
  (71 shorter events, 33.1 us)
Async XLA Ops:
  7.9 20.7 %copy-start.13 = (bf16[2,128,128]{2,1,0:T(8,128)(2,1)}, bf16[2,128,128]{2,1,0:T(8,128)(2,1)S(1)}, u32[]{:S(2)}) copy-start(bf16[2,128,128]{2,1,0:T(8,128)(2,1)S(1)} %pad_maximum_fusion.2) | copy-start | bytes 196612
  8.0 19.4 %collective-permute-start = (bf16[2,128,128]{2,1,0:T(8,128)(2,1)S(1)}, bf16[2,128,128]{2,1,0:T(8,128)(2,1)S(1)}, u32[]{:S(2)}, u32[]{:S(2)}) collective-permute-start(bf16[2,128,128]{2,1,0:T(8,128)(2,1)S(1)} %pad_maximum_fusion.2), channel_id=1, source_target_pairs={{0,0},{8,64},{64,8},{72,72},{1,1},{9,65},{65,9},{73,73},{2,2},{10,... | collective-permute-start | bytes 196616 | tf_op jit(solution)/shard_map/ppermute | solution.py:129
  27.4 8.0 %copy-start.12 = (bf16[1792,128]{1,0:T(8,128)(2,1)S(1)}, bf16[1792,128]{1,0:T(8,128)(2,1)}, u32[]{:S(2)}) copy-start(bf16[1792,128]{1,0:T(8,128)(2,1)} %param.9) | copy-start | bytes 1376260
  28.6 20.8 %all-to-all-start = ((bf16[16,2,128,128]{3,2,1,0:T(8,128)(2,1)}), bf16[16,2,128,128]{3,2,1,0:T(8,128)(2,1)S(1)}, u32[]{:S(2)}, u32[]{:S(2)}) async-start(bf16[16,2,128,128]{3,2,1,0:T(8,128)(2,1)} %broadcast_in_dim.26), calls=%async_computation | async-start | bytes 2097152 | tf_op jit(solution)/shard_map/all_to_all | solution.py:116
  35.4 103.4 %reduce-scatter.4.cloned.1.call-start = ((), (), s32[]{:S(2)}) async-start(), calls=%async_computation.5 | async-start | bytes 6127616 | tf_op jit(solution)/shard_map/reduce_scatter | solution.py:159
  36.6 14.8 %collective-permute-start.2 = (bf16[128,1344]{1,0:T(8,128)(2,1)}, bf16[128,1344]{1,0:T(8,128)(2,1)}, u32[]{:S(2)}, u32[]{:S(2)}) collective-permute-start(bf16[128,1344]{1,0:T(8,128)(2,1)} %bitcast.10), channel_id=1, source_target_pairs={{0,128},{128,256},{256,384},{384,0},{1,129},{129,257},{257,385},{3... | collective-permute-start | bytes 1032200 | tf_op jit(solution)/shard_map/ppermute | solution.py:142
  40.8 13.6 %collective-permute-start.3 = (bf16[128,1344]{1,0:T(8,128)(2,1)}, bf16[128,1344]{1,0:T(8,128)(2,1)}, u32[]{:S(2)}, u32[]{:S(2)}) collective-permute-start(bf16[128,1344]{1,0:T(8,128)(2,1)} %bitcast.12), channel_id=1, source_target_pairs={{0,256},{128,384},{256,0},{384,128},{1,257},{129,385},{257,1},{385... | collective-permute-start | bytes 1032200 | tf_op jit(solution)/shard_map/ppermute | solution.py:142
  46.0 9.4 %collective-permute-start.4 = (bf16[128,1344]{1,0:T(8,128)(2,1)}, bf16[128,1344]{1,0:T(8,128)(2,1)}, u32[]{:S(2)}, u32[]{:S(2)}) collective-permute-start(bf16[128,1344]{1,0:T(8,128)(2,1)} %bitcast.14), channel_id=1, source_target_pairs={{0,384},{128,0},{256,128},{384,256},{1,385},{129,1},{257,129},{385... | collective-permute-start | bytes 1032200 | tf_op jit(solution)/shard_map/ppermute | solution.py:142
  49.4 6.9 %collective-permute-start.1 = (bf16[4,4,2,128,128]{4,3,2,1,0:T(8,128)(2,1)S(1)}, bf16[4,4,2,128,128]{4,3,2,1,0:T(8,128)(2,1)S(1)}, u32[]{:S(2)}, u32[]{:S(2)}) collective-permute-start(bf16[4,4,2,128,128]{4,3,2,1,0:T(8,128)(2,1)S(1)} %bitcast.44), channel_id=1, source_target_pairs={{0,8},{8,0},{1,9},{9,1},{2,10},{10,2},{3,11},{11,3},{4,12},{12,4},... | collective-permute-start | bytes 3145736 | tf_op jit(solution)/shard_map/ppermute | solution.py:21
  56.4 1.9 copy-start.3
  58.3 2.5 copy-start.2
  60.9 153.6 %all-gather.2.cloned.1.call-start = ((), (), s32[]{:S(2)}) async-start(), calls=%async_computation.4 | async-start | bytes 3063808 | tf_op jit(solution)/shard_map/all_gather | solution.py:176
  61.7 13.8 %collective-permute-start.5 = (bf16[2,128,128]{2,1,0:T(8,128)(2,1)S(1)}, bf16[2,128,128]{2,1,0:T(8,128)(2,1)S(1)}, u32[]{:S(2)}, u32[]{:S(2)}) collective-permute-start(bf16[2,128,128]{2,1,0:T(8,128)(2,1)S(1)} %copy-done.14), channel_id=1, source_target_pairs={{0,64},{8,0},{64,72},{72,8},{1,65},{9,1},{65,73},{73,9},{2,66},{10... | collective-permute-start | bytes 196616 | tf_op jit(solution)/shard_map/ppermute | solution.py:163
  97.2 7.3 %collective-permute-start.6 = (bf16[4,4,2,128,128]{4,3,2,1,0:T(8,128)(2,1)S(1)}, bf16[4,4,2,128,128]{4,3,2,1,0:T(8,128)(2,1)S(1)}, u32[]{:S(2)}, u32[]{:S(2)}) collective-permute-start(bf16[4,4,2,128,128]{4,3,2,1,0:T(8,128)(2,1)S(1)} %bitcast.49), channel_id=1, source_target_pairs={{0,8},{8,0},{1,9},{9,1},{2,10},{10,2},{3,11},{11,3},{4,12},{12,4},... | collective-permute-start | bytes 3145736 | tf_op jit(solution)/shard_map/ppermute | solution.py:21
  214.5 1.8 copy-start
  217.6 18.1 %copy-start.1 = (bf16[1024,1344]{1,0:T(8,128)(2,1)S(1)}, bf16[1024,1344]{1,0:T(8,128)(2,1)}, u32[]{:S(2)}) copy-start(bf16[1024,1344]{1,0:T(8,128)(2,1)} %all-gather.2.cloned.1.call-done) | copy-start | bytes 8257540
  220.0 15.7 %collective-permute-start.7 = (f32[2,512,512]{2,1,0:T(8,128)}, f32[2,512,512]{2,1,0:T(8,128)}, u32[]{:S(2)}, u32[]{:S(2)}) collective-permute-start(f32[2,512,512]{2,1,0:T(8,128)} %shard_map.93), channel_id=1, source_target_pairs={{0,8},{8,0},{1,9},{9,1},{2,10},{10,2},{3,11},{11,3},{4,12},{12,4},... | collective-permute-start | bytes 6291464 | tf_op jit(solution)/shard_map/ppermute | solution.py:21
  235.8 1.4 copy-start.5
  240.7 21.6 %all-to-all-start.2 = ((bf16[16,2,128,128]{3,2,1,0:T(8,128)(2,1)}), bf16[16,2,128,128]{3,2,1,0:T(8,128)(2,1)}, u32[]{:S(2)}, u32[]{:S(2)}) async-start(bf16[16,2,128,128]{3,2,1,0:T(8,128)(2,1)} %bitcast.48), calls=%async_computation.2 | async-start | bytes 2097152 | tf_op jit(solution)/shard_map/all_to_all | solution.py:196
  249.9 2.6 copy-start.10
  249.9 3.6 %copy-start.9 = (bf16[1024,224]{1,0:T(8,128)(2,1)S(1)}, bf16[1024,224]{1,0:T(8,128)(2,1)}, u32[]{:S(2)}) copy-start(bf16[1024,224]{1,0:T(8,128)(2,1)} %get-tuple-element.21) | copy-start | bytes 1376260
  251.2 3.3 %copy-start.8 = (bf16[1024,224]{1,0:T(8,128)(2,1)S(1)}, bf16[1024,224]{1,0:T(8,128)(2,1)}, u32[]{:S(2)}) copy-start(bf16[1024,224]{1,0:T(8,128)(2,1)} %get-tuple-element.23) | copy-start | bytes 1376260
  263.8 16.9 %collective-permute-start.8 = (bf16[2,128,128]{2,1,0:T(8,128)(2,1)S(1)}, bf16[2,128,128]{2,1,0:T(8,128)(2,1)S(1)}, u32[]{:S(2)}, u32[]{:S(2)}) collective-permute-start(bf16[2,128,128]{2,1,0:T(8,128)(2,1)S(1)} %reduce_sum.12), channel_id=1, source_target_pairs={{0,0},{8,64},{64,8},{72,72},{1,1},{9,65},{65,9},{73,73},{2,2},{10,... | collective-permute-start | bytes 196616 | tf_op jit(solution)/shard_map/ppermute | solution.py:200
  275.3 2.2 copy-start.6
  (4 other events, 4.2 us)
Sparse Core Ops, SparseCore 0:
  61.0 77.7 reduce-scatter.3
  141.4 72.9 all-gather.1

commit v3 on v2

v3 whole, which is shorter than its diff:
```python
import functools

import jax
import jax.numpy as jnp
from jax import lax
from jax.experimental import pallas as pl
from jax.experimental.pallas import tpu as pltpu
from jax.sharding import Mesh, PartitionSpec as P

BF = jnp.bfloat16
F32 = jnp.float32
DEPTH = ("zh", "gz")
TURN = [(0, 0), (1, 2), (2, 1), (3, 3)]


def dot(left, right, left_dim, right_dim):
    return lax.dot_general(
        left, right, (((left_dim,), (right_dim,)), ((), ())), preferred_element_type=F32
    )


def swap(value, axis):
    return lax.ppermute(value, axis, [(0, 1), (1, 0)])


def shift(value, by):
    return lax.ppermute(value, DEPTH, [(i, (i + by) % 16) for i in range(16)])


def gather_depth(mine):
    level = lax.axis_index(DEPTH)
    row = level // 4
    quarter = jnp.zeros((4,) + mine.shape, BF)
    quarter = lax.dynamic_update_index_in_dim(quarter, mine, row, 0)
    for by in (2, 1, -1):
        quarter = lax.dynamic_update_index_in_dim(
            quarter, shift(mine, 4 * by), lax.rem(row - by + 4, 4), 0
        )
    every = jnp.zeros((4,) + quarter.shape, BF)
    pieces = (
        (quarter, 0, 0),
        (shift(quarter, 1), 1, 0),
        (shift(quarter, -1), -1, 0),
        (shift(quarter[:2], 2), 2, 0),
        (shift(quarter[2:], -2), 2, 2),
    )
    for value, by, start in pieces:
        at = lax.rem(level - by + 16, 4)
        every = lax.dynamic_update_slice(every, value[:, None], (start, at, 0, 0))
    return every.reshape(16 * mine.shape[0], mine.shape[1])


def take(value, index, dim=0):
    return lax.dynamic_index_in_dim(value, index, dim, keepdims=False)


def tokens_of(ref, array, ys):
    return jnp.concatenate(
        [jnp.concatenate([ref[x, y, array] for x in range(4)], axis=0) for y in ys],
        axis=1,
    )


def partial_kernel(core_ref, own_ref, other_ref, weight_ref, out_ref):
    cols = weight_ref.shape[2] // 3
    tok = own_ref.shape[3]
    weight = weight_ref[...].reshape(-1, 3 * cols)

    def work(ref, k):
        pair = dot(tokens_of(ref, 0, range(4)), weight[:, : 2 * cols], 1, 0)
        last = dot(tokens_of(ref, 1, range(4)), weight[:, 2 * cols :], 1, 0)
        out_ref[:, k, :, : 2 * cols] = pair.reshape(4, tok, 2 * cols)
        out_ref[:, k, :, 2 * cols :] = last.reshape(4, tok, cols)

    for core in range(2):

        @pl.when(core_ref[0] == core)
        def _():
            work(own_ref, core)
            work(other_ref, 1 - core)


def parts_kernel(start, width, which_ref, rows_ref, weight_ref, *rest):
    rows = rows_ref[:, which_ref[0], :, :width].reshape(-1, width)
    weight = weight_ref[:, :, start : start + width].reshape(-1, width)
    value = dot(rows, weight, 1, 1)
    if len(rest) == 1:
        rest[0][...] = value
        return
    got_ref, out_ref = rest
    tok, feat = out_ref.shape[2:]
    value = (value + got_ref[...]).astype(BF)
    for x in range(4):
        for y in range(4):
            out_ref[x, y] = value[x * tok : (x + 1) * tok, y * feat : (y + 1) * feat]


def grads_kernel(place_ref, pieces_ref, rows_ref, gate_ref, up_ref, down_ref):
    part = gate_ref.shape[0]
    zh, core = place_ref[0], place_ref[1]
    width = 2 * pieces_ref.shape[6]

    def side(array, y, parity):
        far = jnp.where(zh == parity, 0, 1)
        rows = []
        for x in range(4):
            for k in range(2):
                other = jnp.where(core == k, 0, 1)
                rows.append(pieces_ref[far, other, x, y, array])
        return jnp.concatenate(rows, axis=0)

    for y in range(4):
        at = slice(y * width, (y + 1) * width)
        right = jnp.concatenate([side(0, y, 0), side(0, y, 1)], axis=1)
        pair = dot(rows_ref[: 2 * part], right, 1, 0).astype(BF)
        gate_ref[:, at] = pair[:part]
        up_ref[:, at] = pair[part:]
        right = jnp.concatenate([side(1, y, 0), side(1, y, 1)], axis=1)
        down_ref[:, at] = dot(rows_ref[2 * part :], right, 1, 0).astype(BF)


def local_call(kernel, shape, scalars, *arrays):
    smem = pl.BlockSpec(memory_space=pltpu.SMEM)
    vmem = pl.BlockSpec(memory_space=pltpu.VMEM)
    return pl.pallas_call(
        kernel,
        out_shape=shape,
        in_specs=[smem] + [vmem] * len(arrays),
        out_specs=jax.tree.map(lambda _: vmem, shape),
        compiler_params=pltpu.CompilerParams(vmem_limit_bytes=40 * 2**20),
        cost_estimate=pl.CostEstimate(flops=0, bytes_accessed=0, transcendentals=0),
    )(scalars, *arrays)


def gather_plane(both):
    both = jnp.broadcast_to(both[None], (16,) + both.shape)
    own = lax.all_to_all(both, ("x", "y"), 0, 0, tiled=True)
    own = own.reshape((4, 4) + own.shape[1:])
    return own, swap(own, "c")


def per_device(tokens, cotangent, gate_weight, up_weight, down_weight):
    x, zh, core = (lax.axis_index(name) for name in ("x", "zh", "c"))
    tok, feat = tokens.shape
    cols = gate_weight.shape[1] // 4
    wide = 3 * cols

    both = jnp.stack([tokens, cotangent])

    mixed = jnp.concatenate(
        [
            gate_weight.reshape(tok, 4, cols),
            up_weight.reshape(tok, 4, cols),
            down_weight.T.reshape(tok, 4, cols),
        ],
        axis=2,
    ).transpose(1, 0, 2)
    near = lax.ppermute(both, ("zh", "c"), TURN)
    weight = jnp.zeros_like(mixed)
    weight = lax.dynamic_update_index_in_dim(weight, take(mixed, x), x, 0)
    for by in (1, 2, 3):
        sent = lax.ppermute(
            take(mixed, lax.rem(x + by, 4)), "x", [(i, (i + by) % 4) for i in range(4)]
        )
        weight = lax.dynamic_update_index_in_dim(weight, sent, lax.rem(x + 4 - by, 4), 0)

    own, other = gather_plane(near)

    part = local_call(
        partial_kernel,
        jax.ShapeDtypeStruct((4, 2, tok, wide), F32),
        jnp.stack([core]),
        own,
        other,
        weight,
    )
    both, part = lax.optimization_barrier((both, part))
    total = lax.psum_scatter(
        part.reshape(8 * tok, wide), DEPTH, scatter_dimension=0, tiled=True
    )

    far = lax.ppermute(both, ("zh", "c"), [(0, 2), (1, 0), (2, 3), (3, 1)])
    pieces = jnp.stack([own, other, *gather_plane(far)])
    pieces = pieces.reshape((2, 2) + own.shape)

    gate, upper, hidden_grad = (total[:, i * cols : (i + 1) * cols] for i in range(3))
    sigma = jax.nn.sigmoid(gate)
    activated = gate * sigma
    hidden = (activated * upper).astype(BF)
    gate_delta = (hidden_grad * upper * sigma * (1.0 + gate * (1.0 - sigma))).astype(BF)
    up_delta = (hidden_grad * activated).astype(BF)
    mine = jnp.concatenate([gate_delta, up_delta, hidden], axis=1)
    mine, hidden, pieces = lax.optimization_barrier((mine, hidden, pieces))
    every = lax.all_gather(mine, DEPTH, axis=0, tiled=True)
    hidden = gather_depth(hidden)

    def reduced(rows, start, width):
        rows = rows.reshape(4, 2, tok, rows.shape[1])
        kernel = functools.partial(parts_kernel, start, width)
        give = local_call(
            kernel,
            jax.ShapeDtypeStruct((4 * tok, 4 * feat), F32),
            jnp.stack([1 - core]),
            rows,
            weight,
        )
        sums = local_call(
            kernel,
            jax.ShapeDtypeStruct((4, 4, tok, feat), BF),
            jnp.stack([core]),
            rows,
            weight,
            swap(give, "c"),
        )
        return sums.reshape(16, tok, feat)

    def over_plane(sums):
        sums = lax.all_to_all(sums, ("x", "y"), 0, 0, tiled=True)
        return jnp.sum(sums.astype(F32), axis=0).astype(BF)

    half = cols // 2
    place = jnp.stack([zh, core])
    grad = jax.ShapeDtypeStruct((half, 8 * feat), BF)

    def own_half(rows):
        return jnp.concatenate(
            [
                jnp.where(
                    zh == 0, rows[:, at : at + half], rows[:, at + half : at + cols]
                )
                for at in range(0, rows.shape[1], cols)
            ],
            axis=1,
        ).T

    output = over_plane(reduced(hidden, 2 * cols, cols))
    every, output = lax.optimization_barrier((every, output))
    input_grad = over_plane(reduced(every, 0, 2 * cols))
    gate_grad, up_grad, down_grad = local_call(
        grads_kernel, (grad, grad, grad), place, pieces, own_half(every)
    )
    result = jnp.stack([output, input_grad])
    result, gate_grad, up_grad, down_grad = lax.optimization_barrier(
        (result, gate_grad, up_grad, down_grad)
    )
    result = lax.ppermute(result, ("zh", "c"), TURN)
    return result[0], result[1], gate_grad.T, up_grad.T, down_grad


def solution(mesh):
    fine = Mesh(mesh.devices.reshape(4, 2, 4, 2, 8), ("x", "zh", "y", "c", "gz"))
    gx, gy = ("x", "zh"), ("y", "c")
    act = P(gx, ("gz",) + gy)
    return jax.shard_map(
        per_device,
        mesh=fine,
        in_specs=(act, act, P(("gz",) + gx, gy), P(("gz",) + gx, gy), P(gy, ("gz",) + gx)),
        out_specs=(act, act, P("gz", gy + gx), P("gz", gy + gx), P(gy + gx, "gz")),
        check_vma=False,
    )
```

time: 289 us -> 278 us (0.962)
  waiting for transfers between devices: 132 us -> 73.9 us
  starting transfers between devices: 72.9 us -> 111 us
  blocking collectives: 21.5 us -> 38.1 us
  local copies, waits for them, and re-layouts: 30.7 us -> 23.6 us
    all_gather x1, waiting for transfers between devices: 73.7 us -> 1.13 us  [per_device(): every = lax.all_gather(mine, DEPTH, axis=0, tiled=True)]
    ppermute x0 -> x7, starting transfers between devices: none -> 32.6 us  [shift(): return lax.ppermute(value, DEPTH, [(i, (i + by) % 16) for i in range(16)])]
    all_to_all x0 -> x1, blocking collectives: none -> 16.6 us  [over_plane(): sums = lax.all_to_all(sums, ('x', 'y'), 0, 0, tiled=True)]
    ppermute x0 -> x7, waiting for transfers between devices: none -> 13.6 us  [shift(): return lax.ppermute(value, DEPTH, [(i, (i + by) % 16) for i in range(16)])]
    unnamed x38 -> x16, local copies, waits for them, and re-layouts: 19.1 us -> 9.56 us
    ppermute x3 -> x4, starting transfers between devices: 18.6 us -> 27.7 us  [swap(): return lax.ppermute(value, axis, [(0, 1), (1, 0)])]
    all_to_all x1, waiting for transfers between devices: 6.67 us -> 0.01 us  [over_plane(): sums = lax.all_to_all(sums, ('x', 'y'), 0, 0, tiled=True)]
    ppermute x1, waiting for transfers between devices: 0.01 us -> 5.91 us  [per_device(): result = lax.ppermute(result, ('zh', 'c'), TURN)]
  transfers between devices with their start and end apart: 13 -> 21, of which waited for: 7 -> 11; matrix products, arithmetic and copies ran while one was open for 7% -> 7% of each run, Pallas kernels for 1% -> 1%
where the time goes in v3:
time: 278 us; the launch traced here: 277 us
  starting transfers between devices  111 us (40%)
  waiting for transfers between devices  73.9 us (27%)
  blocking collectives  38.1 us (14%)
  local copies, waits for them, and re-layouts  23.6 us (8%)
  between operations  14.6 us (5%)
  Pallas kernels  8.31 us (3%)
  other arithmetic  7.31 us (3%)
    ppermute x7, starting transfers between devices, shift(): return lax.ppermute(value, DEPTH, [(i, (i + by) % 16) for i in range(16)])  32.6 us
    reduce_scatter x1, waiting for transfers between devices, per_device(): lax.psum_scatter(part.reshape(8 * tok, wide), DEPTH, scatter_dimension=0,...  32.4 us
    ppermute x4, starting transfers between devices, swap(): return lax.ppermute(value, axis, [(0, 1), (1, 0)])  27.7 us
    all_to_all x1, blocking collectives, gather_plane(): own = lax.all_to_all(both, ('x', 'y'), 0, 0, tiled=True)  21.5 us
    ppermute x1, starting transfers between devices, per_device(): near = lax.ppermute(both, ('zh', 'c'), TURN)  16.8 us
    all_to_all x1, blocking collectives, over_plane(): sums = lax.all_to_all(sums, ('x', 'y'), 0, 0, tiled=True)  16.6 us
    ppermute x7, waiting for transfers between devices, shift(): return lax.ppermute(value, DEPTH, [(i, (i + by) % 16) for i in range(16)])  13.6 us
    ppermute x1, waiting for transfers between devices, per_device(): far = lax.ppermute(both, ('zh', 'c'), [(0, 2), (1, 0), (2, 3), (3, 1)])  12.1 us
  transfers between devices with their start and end apart: 21, of which 11 were waited for; matrix products, arithmetic and copies ran while one was open for 7% of the time, Pallas kernels for 1%

profile of v3, /device:TPU:1, one launch (start us, length us, event | category | flops | bytes accessed | tf_op | source)
XLA Modules:
  0.0 276.9 jit_solution(13121521391077220082)
XLA Ops:
  8.0 16.8 %collective-permute-start = (bf16[2,128,128]{2,1,0:T(8,128)(2,1)S(1)}, bf16[2,128,128]{2,1,0:T(8,128)(2,1)S(1)}, u32[]{:S(2)}, u32[]{:S(2)}) collective-permute-start(bf16[2,128,128]{2,1,0:T(8,128)(2,1)S(1)} %pad_maximum_fusion.2), channel_id=1, source_target_pairs={{0,0},{8,64},{64,8},{72,72},{1,1},{9,65},{65,9},{73,73},{2,2},{10,... | collective-permute-start | bytes 196616 | tf_op jit(solution)/shard_map/ppermute | solution.py:158
  28.6 6.8 %all-to-all-start = ((bf16[16,2,128,128]{3,2,1,0:T(8,128)(2,1)}), bf16[16,2,128,128]{3,2,1,0:T(8,128)(2,1)S(1)}, u32[]{:S(2)}, u32[]{:S(2)}) async-start(bf16[16,2,128,128]{3,2,1,0:T(8,128)(2,1)} %broadcast_in_dim.60), calls=%async_computation | async-start | bytes 2097152 | tf_op jit(solution)/shard_map/all_to_all | solution.py:137
  36.6 3.3 %collective-permute-start.2 = (bf16[128,1344]{1,0:T(8,128)(2,1)}, bf16[128,1344]{1,0:T(8,128)(2,1)}, u32[]{:S(2)}, u32[]{:S(2)}) collective-permute-start(bf16[128,1344]{1,0:T(8,128)(2,1)} %bitcast.10), channel_id=1, source_target_pairs={{0,128},{128,256},{256,384},{384,0},{1,129},{129,257},{257,385},{3... | collective-permute-start | bytes 1032200 | tf_op jit(solution)/shard_map/ppermute | solution.py:162
  40.8 4.3 %collective-permute-start.3 = (bf16[128,1344]{1,0:T(8,128)(2,1)}, bf16[128,1344]{1,0:T(8,128)(2,1)}, u32[]{:S(2)}, u32[]{:S(2)}) collective-permute-start(bf16[128,1344]{1,0:T(8,128)(2,1)} %bitcast.12), channel_id=1, source_target_pairs={{0,256},{128,384},{256,0},{384,128},{1,257},{129,385},{257,1},{385... | collective-permute-start | bytes 1032200 | tf_op jit(solution)/shard_map/ppermute | solution.py:162
  46.0 3.1 %collective-permute-start.4 = (bf16[128,1344]{1,0:T(8,128)(2,1)}, bf16[128,1344]{1,0:T(8,128)(2,1)}, u32[]{:S(2)}, u32[]{:S(2)}) collective-permute-start(bf16[128,1344]{1,0:T(8,128)(2,1)} %bitcast.14), channel_id=1, source_target_pairs={{0,384},{128,0},{256,128},{384,256},{1,385},{129,1},{257,129},{385... | collective-permute-start | bytes 1032200 | tf_op jit(solution)/shard_map/ppermute | solution.py:162
  62.8 12.1 %collective-permute-done.5 = bf16[2,128,128]{2,1,0:T(8,128)(2,1)S(1)} collective-permute-done((bf16[2,128,128]{2,1,0:T(8,128)(2,1)}, bf16[2,128,128]{2,1,0:T(8,128)(2,1)S(1)}, u32[]{:S(2)}, u32[]{:S(2)}) %collective-permute-start.5) | collective-permute-done | bytes 65568 | tf_op jit(solution)/shard_map/ppermute | solution.py:182
  75.2 21.5 %all_to_all.20 = bf16[16,2,128,128]{3,2,1,0:T(8,128)(2,1)S(1)} all-to-all(bf16[16,2,128,128]{3,2,1,0:T(8,128)(2,1)S(1)} %broadcast_in_dim.65), channel_id=1, replica_groups=mesh['x'=4,'zh'=2,'y'=4,'c'=2,'gz'=8] {'x','y'}, dimensions={0} | all-to-all | bytes 2097152 | tf_op jit(solution)/shard_map/all_to_all | solution.py:137
  96.7 5.0 %collective-permute-start.6 = (bf16[4,4,2,128,128]{4,3,2,1,0:T(8,128)(2,1)S(1)}, bf16[4,4,2,128,128]{4,3,2,1,0:T(8,128)(2,1)S(1)}, u32[]{:S(2)}, u32[]{:S(2)}) collective-permute-start(bf16[4,4,2,128,128]{4,3,2,1,0:T(8,128)(2,1)S(1)} %bitcast.83), channel_id=1, source_target_pairs={{0,8},{8,0},{1,9},{9,1},{2,10},{10,2},{3,11},{11,3},{4,12},{12,4},... | collective-permute-start | bytes 3145736 | tf_op jit(solution)/shard_map/ppermute | solution.py:23
  106.3 32.4 %reduce-scatter.4.cloned.1.call-done = f32[64,1344]{1,0:T(8,128)} async-done(((f32[1024,1344]{1,0:T(8,128)}), f32[64,1344]{1,0:T(8,128)}) %reduce-scatter.4.cloned.1.call-update) | async-done | bytes 344080 | tf_op jit(solution)/shard_map/reduce_scatter | solution.py:178
  140.8 9.5 %collective-permute-start.7 = (bf16[64,448]{1,0:T(8,128)(2,1)S(1)}, bf16[64,448]{1,0:T(8,128)(2,1)S(1)}, u32[]{:S(2)}, u32[]{:S(2)}) collective-permute-start(bf16[64,448]{1,0:T(8,128)(2,1)S(1)} %get-tuple-element.22), channel_id=1, source_target_pairs={{0,64},{1,65},{2,66},{3,67},{4,68},{5,69},{6,70},{7,71},{64,0},{65... | collective-permute-start | bytes 172040 | tf_op jit(solution)/shard_map/ppermute | solution.py:27
  150.2 3.6 %collective-permute-start.8 = (bf16[64,448]{1,0:T(8,128)(2,1)S(1)}, bf16[64,448]{1,0:T(8,128)(2,1)S(1)}, u32[]{:S(2)}, u32[]{:S(2)}) collective-permute-start(bf16[64,448]{1,0:T(8,128)(2,1)S(1)} %get-tuple-element.22), channel_id=1, source_target_pairs={{0,4},{1,5},{2,6},{3,7},{4,64},{5,65},{6,66},{7,67},{64,68},{65,69... | collective-permute-start | bytes 172040 | tf_op jit(solution)/shard_map/ppermute | solution.py:27
  153.9 5.6 %collective-permute-start.9 = (bf16[64,448]{1,0:T(8,128)(2,1)S(1)}, bf16[64,448]{1,0:T(8,128)(2,1)S(1)}, u32[]{:S(2)}, u32[]{:S(2)}) collective-permute-start(bf16[64,448]{1,0:T(8,128)(2,1)S(1)} %get-tuple-element.22), channel_id=1, source_target_pairs={{0,68},{1,69},{2,70},{3,71},{4,0},{5,1},{6,2},{7,3},{64,4},{65,5},... | collective-permute-start | bytes 172040 | tf_op jit(solution)/shard_map/ppermute | solution.py:27
  159.6 7.7 %collective-permute-done.9 = bf16[64,448]{1,0:T(8,128)(2,1)S(1)} collective-permute-done((bf16[64,448]{1,0:T(8,128)(2,1)S(1)}, bf16[64,448]{1,0:T(8,128)(2,1)S(1)}, u32[]{:S(2)}, u32[]{:S(2)}) %collective-permute-start.9) | collective-permute-done | bytes 57376 | tf_op jit(solution)/shard_map/ppermute | solution.py:27
  169.7 4.2 %collective-permute-start.11 = (bf16[4,64,448]{2,1,0:T(8,128)(2,1)S(1)}, bf16[4,64,448]{2,1,0:T(8,128)(2,1)S(1)}, u32[]{:S(2)}, u32[]{:S(2)}) collective-permute-start(bf16[4,64,448]{2,1,0:T(8,128)(2,1)S(1)} %bitcast_dynamic-update-slice_fusion.9), channel_id=1, source_target_pairs={{0,71},{1,0},{2,1},{3,2},{4,3},{5,4},{6,5},{7,6},{64,7},{65,64},{6... | collective-permute-start | bytes 688136 | tf_op jit(solution)/shard_map/ppermute | solution.py:27
  175.8 5.5 %collective-permute-start.13 = (bf16[2,64,448]{2,1,0:T(8,128)(2,1)S(1)}, bf16[2,64,448]{2,1,0:T(8,128)(2,1)S(1)}, u32[]{:S(2)}, u32[]{:S(2)}) collective-permute-start(bf16[2,64,448]{2,1,0:T(8,128)(2,1)S(1)} %get-tuple-element.43), channel_id=1, source_target_pairs={{0,70},{1,71},{2,0},{3,1},{4,2},{5,3},{6,4},{7,5},{64,6},{65,7},{6... | collective-permute-start | bytes 344072 | tf_op jit(solution)/shard_map/ppermute | solution.py:27
  181.5 4.8 %collective-permute-done.12 = bf16[2,64,448]{2,1,0:T(8,128)(2,1)S(1)} collective-permute-done((bf16[2,64,448]{2,1,0:T(8,128)(2,1)S(1)}, bf16[2,64,448]{2,1,0:T(8,128)(2,1)S(1)}, u32[]{:S(2)}, u32[]{:S(2)}) %collective-permute-start.12) | collective-permute-done | bytes 114720 | tf_op jit(solution)/shard_map/ppermute | solution.py:27
  187.8 11.3 %collective-permute-start.14 = (f32[512,512]{1,0:T(8,128)S(1)}, f32[512,512]{1,0:T(8,128)S(1)}, u32[]{:S(2)}, u32[]{:S(2)}) collective-permute-start(f32[512,512]{1,0:T(8,128)S(1)} %shard_map.93), channel_id=1, source_target_pairs={{0,8},{8,0},{1,9},{9,1},{2,10},{10,2},{3,11},{11,3},{4,12},{12,4},... | collective-permute-start | bytes 3145736 | tf_op jit(solution)/shard_map/ppermute | solution.py:23
  201.9 16.6 %all_to_all.21 = bf16[16,128,128]{2,1,0:T(8,128)(2,1)S(1)} all-to-all(bf16[16,128,128]{2,1,0:T(8,128)(2,1)S(1)} %bitcast.82), channel_id=1, replica_groups=mesh['x'=4,'zh'=2,'y'=4,'c'=2,'gz'=8] {'x','y'}, dimensions={0} | all-to-all | bytes 1048576 | tf_op jit(solution)/shard_map/all_to_all | solution.py:218
  222.8 9.4 %collective-permute-start.15 = (f32[512,512]{1,0:T(8,128)S(1)}, f32[512,512]{1,0:T(8,128)S(1)}, u32[]{:S(2)}, u32[]{:S(2)}) collective-permute-start(f32[512,512]{1,0:T(8,128)S(1)} %shard_map.95), channel_id=1, source_target_pairs={{0,8},{8,0},{1,9},{9,1},{2,10},{10,2},{3,11},{11,3},{4,12},{12,4},... | collective-permute-start | bytes 3145736 | tf_op jit(solution)/shard_map/ppermute | solution.py:23
  237.9 6.2 %all-to-all-start.3 = ((bf16[16,128,128]{2,1,0:T(8,128)(2,1)}), bf16[16,128,128]{2,1,0:T(8,128)(2,1)S(1)}, u32[]{:S(2)}, u32[]{:S(2)}) async-start(bf16[16,128,128]{2,1,0:T(8,128)(2,1)} %bitcast.42), calls=%async_computation.3 | async-start | bytes 1048576 | tf_op jit(solution)/shard_map/all_to_all | solution.py:218
  244.2 4.7 %copy.49 = bf16[1024,1344]{0,1:T(8,128)(2,1)} copy(bf16[1024,1344]{1,0:T(8,128)(2,1)} %all-gather.2.cloned.1.call-done) | data formatting | bytes 5505024 | tf_op jit(solution)/shard_map/optimization_barrier | solution.py:237
  251.8 3.2 %shard_map.97 = (bf16[224,1024]{1,0:T(8,128)(2,1)}, bf16[224,1024]{1,0:T(8,128)(2,1)}, bf16[224,1024]{1,0:T(8,128)(2,1)}) custom-call(s32[2]{0:T(128)S(1)} %pad_add_fusion.place_ref, bf16[2,2,4,4,2,128,128]{6,5,4,3,2,1,0:T(8,128)(2,1)S(1)} %bitcast.75, bf16[672,1024]{1,0:T(8,128)(2,1)S(1)} %maximum_bitcast_fusion.rows_ref), custom_call_target="tpu_custom_call" | custom-call | tf_op jit(solution)/shard_map/pallas_call | solution.py:125
  255.1 8.4 %collective-permute-start.16 = (bf16[2,128,128]{2,1,0:T(8,128)(2,1)S(1)}, bf16[2,128,128]{2,1,0:T(8,128)(2,1)S(1)}, u32[]{:S(2)}, u32[]{:S(2)}) collective-permute-start(bf16[2,128,128]{2,1,0:T(8,128)(2,1)S(1)} %pad_maximum_fusion.3), channel_id=1, source_target_pairs={{0,0},{8,64},{64,8},{72,72},{1,1},{9,65},{65,9},{73,73},{2,2},{10,... | collective-permute-start | bytes 196616 | tf_op jit(solution)/shard_map/ppermute | solution.py:246
  263.5 5.9 %collective-permute-done.16 = bf16[2,128,128]{2,1,0:T(8,128)(2,1)S(1)} collective-permute-done((bf16[2,128,128]{2,1,0:T(8,128)(2,1)S(1)}, bf16[2,128,128]{2,1,0:T(8,128)(2,1)S(1)}, u32[]{:S(2)}, u32[]{:S(2)}) %collective-permute-start.16) | collective-permute-done | bytes 65568 | tf_op jit(solution)/shard_map/ppermute | solution.py:246
  (81 shorter events, 50.6 us)
Async XLA Ops:
  7.9 20.7 %copy-start.6 = (bf16[2,128,128]{2,1,0:T(8,128)(2,1)}, bf16[2,128,128]{2,1,0:T(8,128)(2,1)S(1)}, u32[]{:S(2)}) copy-start(bf16[2,128,128]{2,1,0:T(8,128)(2,1)S(1)} %pad_maximum_fusion.2) | copy-start | bytes 196612
  8.0 19.4 %collective-permute-start = (bf16[2,128,128]{2,1,0:T(8,128)(2,1)S(1)}, bf16[2,128,128]{2,1,0:T(8,128)(2,1)S(1)}, u32[]{:S(2)}, u32[]{:S(2)}) collective-permute-start(bf16[2,128,128]{2,1,0:T(8,128)(2,1)S(1)} %pad_maximum_fusion.2), channel_id=1, source_target_pairs={{0,0},{8,64},{64,8},{72,72},{1,1},{9,65},{65,9},{73,73},{2,2},{10,... | collective-permute-start | bytes 196616 | tf_op jit(solution)/shard_map/ppermute | solution.py:158
  27.4 8.1 %copy-start.4 = (bf16[1792,128]{1,0:T(8,128)(2,1)S(1)}, bf16[1792,128]{1,0:T(8,128)(2,1)}, u32[]{:S(2)}) copy-start(bf16[1792,128]{1,0:T(8,128)(2,1)} %param.9) | copy-start | bytes 1376260
  28.6 20.8 %all-to-all-start = ((bf16[16,2,128,128]{3,2,1,0:T(8,128)(2,1)}), bf16[16,2,128,128]{3,2,1,0:T(8,128)(2,1)S(1)}, u32[]{:S(2)}, u32[]{:S(2)}) async-start(bf16[16,2,128,128]{3,2,1,0:T(8,128)(2,1)} %broadcast_in_dim.60), calls=%async_computation | async-start | bytes 2097152 | tf_op jit(solution)/shard_map/all_to_all | solution.py:137
  35.4 103.3 %reduce-scatter.4.cloned.1.call-start = ((), (), s32[]{:S(2)}) async-start(), calls=%async_computation.6 | async-start | bytes 6127616 | tf_op jit(solution)/shard_map/reduce_scatter | solution.py:178
  36.6 14.8 %collective-permute-start.2 = (bf16[128,1344]{1,0:T(8,128)(2,1)}, bf16[128,1344]{1,0:T(8,128)(2,1)}, u32[]{:S(2)}, u32[]{:S(2)}) collective-permute-start(bf16[128,1344]{1,0:T(8,128)(2,1)} %bitcast.10), channel_id=1, source_target_pairs={{0,128},{128,256},{256,384},{384,0},{1,129},{129,257},{257,385},{3... | collective-permute-start | bytes 1032200 | tf_op jit(solution)/shard_map/ppermute | solution.py:162
  40.8 13.6 %collective-permute-start.3 = (bf16[128,1344]{1,0:T(8,128)(2,1)}, bf16[128,1344]{1,0:T(8,128)(2,1)}, u32[]{:S(2)}, u32[]{:S(2)}) collective-permute-start(bf16[128,1344]{1,0:T(8,128)(2,1)} %bitcast.12), channel_id=1, source_target_pairs={{0,256},{128,384},{256,0},{384,128},{1,257},{129,385},{257,1},{385... | collective-permute-start | bytes 1032200 | tf_op jit(solution)/shard_map/ppermute | solution.py:162
  46.0 9.4 %collective-permute-start.4 = (bf16[128,1344]{1,0:T(8,128)(2,1)}, bf16[128,1344]{1,0:T(8,128)(2,1)}, u32[]{:S(2)}, u32[]{:S(2)}) collective-permute-start(bf16[128,1344]{1,0:T(8,128)(2,1)} %bitcast.14), channel_id=1, source_target_pairs={{0,384},{128,0},{256,128},{384,256},{1,385},{129,1},{257,129},{385... | collective-permute-start | bytes 1032200 | tf_op jit(solution)/shard_map/ppermute | solution.py:162
  49.5 6.9 %collective-permute-start.1 = (bf16[4,4,2,128,128]{4,3,2,1,0:T(8,128)(2,1)S(1)}, bf16[4,4,2,128,128]{4,3,2,1,0:T(8,128)(2,1)S(1)}, u32[]{:S(2)}, u32[]{:S(2)}) collective-permute-start(bf16[4,4,2,128,128]{4,3,2,1,0:T(8,128)(2,1)S(1)} %bitcast.76), channel_id=1, source_target_pairs={{0,8},{8,0},{1,9},{9,1},{2,10},{10,2},{3,11},{11,3},{4,12},{12,4},... | collective-permute-start | bytes 3145736 | tf_op jit(solution)/shard_map/ppermute | solution.py:23
  60.8 159.4 %all-gather.2.cloned.1.call-start = ((), (), s32[]{:S(2)}) async-start(), calls=%async_computation.5 | async-start | bytes 3063808 | tf_op jit(solution)/shard_map/all_gather | solution.py:194
  60.9 14.0 %collective-permute-start.5 = (bf16[2,128,128]{2,1,0:T(8,128)(2,1)}, bf16[2,128,128]{2,1,0:T(8,128)(2,1)S(1)}, u32[]{:S(2)}, u32[]{:S(2)}) collective-permute-start(bf16[2,128,128]{2,1,0:T(8,128)(2,1)} %copy-done.6), channel_id=1, source_target_pairs={{0,64},{8,0},{64,72},{72,8},{1,65},{9,1},{65,73},{73,9},{2,66},{10... | collective-permute-start | bytes 196616 | tf_op jit(solution)/shard_map/ppermute | solution.py:182
  96.7 7.3 %collective-permute-start.6 = (bf16[4,4,2,128,128]{4,3,2,1,0:T(8,128)(2,1)S(1)}, bf16[4,4,2,128,128]{4,3,2,1,0:T(8,128)(2,1)S(1)}, u32[]{:S(2)}, u32[]{:S(2)}) collective-permute-start(bf16[4,4,2,128,128]{4,3,2,1,0:T(8,128)(2,1)S(1)} %bitcast.83), channel_id=1, source_target_pairs={{0,8},{8,0},{1,9},{9,1},{2,10},{10,2},{3,11},{11,3},{4,12},{12,4},... | collective-permute-start | bytes 3145736 | tf_op jit(solution)/shard_map/ppermute | solution.py:23
  140.8 18.8 %collective-permute-start.7 = (bf16[64,448]{1,0:T(8,128)(2,1)S(1)}, bf16[64,448]{1,0:T(8,128)(2,1)S(1)}, u32[]{:S(2)}, u32[]{:S(2)}) collective-permute-start(bf16[64,448]{1,0:T(8,128)(2,1)S(1)} %get-tuple-element.22), channel_id=1, source_target_pairs={{0,64},{1,65},{2,66},{3,67},{4,68},{5,69},{6,70},{7,71},{64,0},{65... | collective-permute-start | bytes 172040 | tf_op jit(solution)/shard_map/ppermute | solution.py:27
  150.2 9.3 %collective-permute-start.8 = (bf16[64,448]{1,0:T(8,128)(2,1)S(1)}, bf16[64,448]{1,0:T(8,128)(2,1)S(1)}, u32[]{:S(2)}, u32[]{:S(2)}) collective-permute-start(bf16[64,448]{1,0:T(8,128)(2,1)S(1)} %get-tuple-element.22), channel_id=1, source_target_pairs={{0,4},{1,5},{2,6},{3,7},{4,64},{5,65},{6,66},{7,67},{64,68},{65,69... | collective-permute-start | bytes 172040 | tf_op jit(solution)/shard_map/ppermute | solution.py:27
  153.9 13.4 %collective-permute-start.9 = (bf16[64,448]{1,0:T(8,128)(2,1)S(1)}, bf16[64,448]{1,0:T(8,128)(2,1)S(1)}, u32[]{:S(2)}, u32[]{:S(2)}) collective-permute-start(bf16[64,448]{1,0:T(8,128)(2,1)S(1)} %get-tuple-element.22), channel_id=1, source_target_pairs={{0,68},{1,69},{2,70},{3,71},{4,0},{5,1},{6,2},{7,3},{64,4},{65,5},... | collective-permute-start | bytes 172040 | tf_op jit(solution)/shard_map/ppermute | solution.py:27
  167.3 14.1 %collective-permute-start.10 = (bf16[4,64,448]{2,1,0:T(8,128)(2,1)S(1)}, bf16[4,64,448]{2,1,0:T(8,128)(2,1)S(1)}, u32[]{:S(2)}, u32[]{:S(2)}) collective-permute-start(bf16[4,64,448]{2,1,0:T(8,128)(2,1)S(1)} %bitcast_dynamic-update-slice_fusion.9), channel_id=1, source_target_pairs={{0,1},{1,2},{2,3},{3,4},{4,5},{5,6},{6,7},{7,64},{64,65},{65,66},{... | collective-permute-start | bytes 688136 | tf_op jit(solution)/shard_map/ppermute | solution.py:27
  169.7 11.8 %collective-permute-start.11 = (bf16[4,64,448]{2,1,0:T(8,128)(2,1)S(1)}, bf16[4,64,448]{2,1,0:T(8,128)(2,1)S(1)}, u32[]{:S(2)}, u32[]{:S(2)}) collective-permute-start(bf16[4,64,448]{2,1,0:T(8,128)(2,1)S(1)} %bitcast_dynamic-update-slice_fusion.9), channel_id=1, source_target_pairs={{0,71},{1,0},{2,1},{3,2},{4,3},{5,4},{6,5},{7,6},{64,7},{65,64},{6... | collective-permute-start | bytes 688136 | tf_op jit(solution)/shard_map/ppermute | solution.py:27
  173.9 12.4 %collective-permute-start.12 = (bf16[2,64,448]{2,1,0:T(8,128)(2,1)S(1)}, bf16[2,64,448]{2,1,0:T(8,128)(2,1)S(1)}, u32[]{:S(2)}, u32[]{:S(2)}) collective-permute-start(bf16[2,64,448]{2,1,0:T(8,128)(2,1)S(1)} %get-tuple-element.44), channel_id=1, source_target_pairs={{0,2},{1,3},{2,4},{3,5},{4,6},{5,7},{6,64},{7,65},{64,66},{65,67},... | collective-permute-start | bytes 344072 | tf_op jit(solution)/shard_map/ppermute | solution.py:27
  175.8 11.5 %collective-permute-start.13 = (bf16[2,64,448]{2,1,0:T(8,128)(2,1)S(1)}, bf16[2,64,448]{2,1,0:T(8,128)(2,1)S(1)}, u32[]{:S(2)}, u32[]{:S(2)}) collective-permute-start(bf16[2,64,448]{2,1,0:T(8,128)(2,1)S(1)} %get-tuple-element.43), channel_id=1, source_target_pairs={{0,70},{1,71},{2,0},{3,1},{4,2},{5,3},{6,4},{7,5},{64,6},{65,7},{6... | collective-permute-start | bytes 344072 | tf_op jit(solution)/shard_map/ppermute | solution.py:27
  187.8 13.6 %collective-permute-start.14 = (f32[512,512]{1,0:T(8,128)S(1)}, f32[512,512]{1,0:T(8,128)S(1)}, u32[]{:S(2)}, u32[]{:S(2)}) collective-permute-start(f32[512,512]{1,0:T(8,128)S(1)} %shard_map.93), channel_id=1, source_target_pairs={{0,8},{8,0},{1,9},{9,1},{2,10},{10,2},{3,11},{11,3},{4,12},{12,4},... | collective-permute-start | bytes 3145736 | tf_op jit(solution)/shard_map/ppermute | solution.py:23
  222.8 11.7 %collective-permute-start.15 = (f32[512,512]{1,0:T(8,128)S(1)}, f32[512,512]{1,0:T(8,128)S(1)}, u32[]{:S(2)}, u32[]{:S(2)}) collective-permute-start(f32[512,512]{1,0:T(8,128)S(1)} %shard_map.95), channel_id=1, source_target_pairs={{0,8},{8,0},{1,9},{9,1},{2,10},{10,2},{3,11},{11,3},{4,12},{12,4},... | collective-permute-start | bytes 3145736 | tf_op jit(solution)/shard_map/ppermute | solution.py:23
  237.9 17.1 %all-to-all-start.3 = ((bf16[16,128,128]{2,1,0:T(8,128)(2,1)}), bf16[16,128,128]{2,1,0:T(8,128)(2,1)S(1)}, u32[]{:S(2)}, u32[]{:S(2)}) async-start(bf16[16,128,128]{2,1,0:T(8,128)(2,1)} %bitcast.42), calls=%async_computation.3 | async-start | bytes 1048576 | tf_op jit(solution)/shard_map/all_to_all | solution.py:218
  251.8 3.2 %copy-start.5 = (bf16[128,128]{1,0:T(8,128)(2,1)S(1)}, bf16[128,128]{1,0:T(8,128)(2,1)}, u32[]{:S(2)}) copy-start(bf16[128,128]{1,0:T(8,128)(2,1)} %reduce_sum.24) | copy-start | bytes 98308
  255.1 14.3 %collective-permute-start.16 = (bf16[2,128,128]{2,1,0:T(8,128)(2,1)S(1)}, bf16[2,128,128]{2,1,0:T(8,128)(2,1)S(1)}, u32[]{:S(2)}, u32[]{:S(2)}) collective-permute-start(bf16[2,128,128]{2,1,0:T(8,128)(2,1)S(1)} %pad_maximum_fusion.3), channel_id=1, source_target_pairs={{0,0},{8,64},{64,8},{72,72},{1,1},{9,65},{65,9},{73,73},{2,2},{10,... | collective-permute-start | bytes 196616 | tf_op jit(solution)/shard_map/ppermute | solution.py:246
  (4 other events, 9.2 us)
Sparse Core Ops, SparseCore 0:
  61.0 77.6 reduce-scatter.3
  141.4 78.8 all-gather.1

commit v4 on v3

--- a/solution.py
+++ b/solution.py
@@ -23,33 +23,6 @@
     return lax.ppermute(value, axis, [(0, 1), (1, 0)])
 
 
-def shift(value, by):
-    return lax.ppermute(value, DEPTH, [(i, (i + by) % 16) for i in range(16)])
-
-
-def gather_depth(mine):
-    level = lax.axis_index(DEPTH)
-    row = level // 4
-    quarter = jnp.zeros((4,) + mine.shape, BF)
-    quarter = lax.dynamic_update_index_in_dim(quarter, mine, row, 0)
-    for by in (2, 1, -1):
-        quarter = lax.dynamic_update_index_in_dim(
-            quarter, shift(mine, 4 * by), lax.rem(row - by + 4, 4), 0
-        )
-    every = jnp.zeros((4,) + quarter.shape, BF)
-    pieces = (
-        (quarter, 0, 0),
-        (shift(quarter, 1), 1, 0),
-        (shift(quarter, -1), -1, 0),
-        (shift(quarter[:2], 2), 2, 0),
-        (shift(quarter[2:], -2), 2, 2),
-    )
-    for value, by, start in pieces:
-        at = lax.rem(level - by + 16, 4)
-        every = lax.dynamic_update_slice(every, value[:, None], (start, at, 0, 0))
-    return every.reshape(16 * mine.shape[0], mine.shape[1])
-
-
 def take(value, index, dim=0):
     return lax.dynamic_index_in_dim(value, index, dim, keepdims=False)
 
@@ -80,22 +53,22 @@
             work(other_ref, 1 - core)
 
 
-def parts_kernel(start, width, which_ref, rows_ref, weight_ref, *rest):
-    rows = rows_ref[:, which_ref[0], :, :width].reshape(-1, width)
+def parts_kernel(start, rows_ref, weight_ref, out_ref):
+    tok, feat = out_ref.shape[3:]
+    width = rows_ref.shape[3]
     weight = weight_ref[:, :, start : start + width].reshape(-1, width)
-    value = dot(rows, weight, 1, 1)
-    if len(rest) == 1:
-        rest[0][...] = value
-        return
-    got_ref, out_ref = rest
-    tok, feat = out_ref.shape[2:]
-    value = (value + got_ref[...]).astype(BF)
     for x in range(4):
+        value = dot(rows_ref[x].reshape(2 * tok, width), weight, 1, 1).astype(BF)
         for y in range(4):
-            out_ref[x, y] = value[x * tok : (x + 1) * tok, y * feat : (y + 1) * feat]
-
-
-def grads_kernel(place_ref, pieces_ref, rows_ref, gate_ref, up_ref, down_ref):
+            for k in range(2):
+                out_ref[x, y, k] = value[
+                    k * tok : (k + 1) * tok, y * feat : (y + 1) * feat
+                ]
+
+
+def grads_kernel(
+    place_ref, pieces_ref, deltas_ref, hidden_ref, gate_ref, up_ref, down_ref
+):
     part = gate_ref.shape[0]
     zh, core = place_ref[0], place_ref[1]
     width = 2 * pieces_ref.shape[6]
@@ -112,24 +85,24 @@
     for y in range(4):
         at = slice(y * width, (y + 1) * width)
         right = jnp.concatenate([side(0, y, 0), side(0, y, 1)], axis=1)
-        pair = dot(rows_ref[: 2 * part], right, 1, 0).astype(BF)
+        pair = dot(deltas_ref[...], right, 1, 0).astype(BF)
         gate_ref[:, at] = pair[:part]
         up_ref[:, at] = pair[part:]
         right = jnp.concatenate([side(1, y, 0), side(1, y, 1)], axis=1)
-        down_ref[:, at] = dot(rows_ref[2 * part :], right, 1, 0).astype(BF)
-
-
-def local_call(kernel, shape, scalars, *arrays):
+        down_ref[:, at] = dot(hidden_ref[...], right, 1, 0).astype(BF)
+
+
+def local_call(kernel, shape, arrays, *scalars):
     smem = pl.BlockSpec(memory_space=pltpu.SMEM)
     vmem = pl.BlockSpec(memory_space=pltpu.VMEM)
     return pl.pallas_call(
         kernel,
         out_shape=shape,
-        in_specs=[smem] + [vmem] * len(arrays),
+        in_specs=[smem] * len(scalars) + [vmem] * len(arrays),
         out_specs=jax.tree.map(lambda _: vmem, shape),
         compiler_params=pltpu.CompilerParams(vmem_limit_bytes=40 * 2**20),
         cost_estimate=pl.CostEstimate(flops=0, bytes_accessed=0, transcendentals=0),
-    )(scalars, *arrays)
+    )(*scalars, *arrays)
 
 
 def gather_plane(both):
@@ -169,10 +142,8 @@
     part = local_call(
         partial_kernel,
         jax.ShapeDtypeStruct((4, 2, tok, wide), F32),
+        (own, other, weight),
         jnp.stack([core]),
-        own,
-        other,
-        weight,
     )
     both, part = lax.optimization_barrier((both, part))
     total = lax.psum_scatter(
@@ -189,33 +160,19 @@
     hidden = (activated * upper).astype(BF)
     gate_delta = (hidden_grad * upper * sigma * (1.0 + gate * (1.0 - sigma))).astype(BF)
     up_delta = (hidden_grad * activated).astype(BF)
-    mine = jnp.concatenate([gate_delta, up_delta, hidden], axis=1)
+    mine = jnp.concatenate([gate_delta, up_delta], axis=1)
     mine, hidden, pieces = lax.optimization_barrier((mine, hidden, pieces))
-    every = lax.all_gather(mine, DEPTH, axis=0, tiled=True)
-    hidden = gather_depth(hidden)
-
-    def reduced(rows, start, width):
-        rows = rows.reshape(4, 2, tok, rows.shape[1])
-        kernel = functools.partial(parts_kernel, start, width)
-        give = local_call(
-            kernel,
-            jax.ShapeDtypeStruct((4 * tok, 4 * feat), F32),
-            jnp.stack([1 - core]),
-            rows,
-            weight,
+    deltas = lax.all_gather(mine, DEPTH, axis=0, tiled=True)
+    hidden = lax.all_gather(hidden, DEPTH, axis=0, tiled=True)
+
+    def reduced(rows, start):
+        sums = local_call(
+            functools.partial(parts_kernel, start),
+            jax.ShapeDtypeStruct((4, 4, 2, tok, feat), BF),
+            (rows.reshape(4, 2, tok, rows.shape[1]), weight),
         )
-        sums = local_call(
-            kernel,
-            jax.ShapeDtypeStruct((4, 4, tok, feat), BF),
-            jnp.stack([core]),
-            rows,
-            weight,
-            swap(give, "c"),
-        )
-        return sums.reshape(16, tok, feat)
-
-    def over_plane(sums):
-        sums = lax.all_to_all(sums, ("x", "y"), 0, 0, tiled=True)
+        sums = sums.reshape(32, tok, feat)
+        sums = lax.all_to_all(sums, ("x", "y", "c"), 0, 0, tiled=True)
         return jnp.sum(sums.astype(F32), axis=0).astype(BF)
 
     half = cols // 2
@@ -233,11 +190,14 @@
             axis=1,
         ).T
 
-    output = over_plane(reduced(hidden, 2 * cols, cols))
-    every, output = lax.optimization_barrier((every, output))
-    input_grad = over_plane(reduced(every, 0, 2 * cols))
+    output = reduced(hidden, 2 * cols)
+    deltas, output = lax.optimization_barrier((deltas, output))
+    input_grad = reduced(deltas, 0)
     gate_grad, up_grad, down_grad = local_call(
-        grads_kernel, (grad, grad, grad), place, pieces, own_half(every)
+        grads_kernel,
+        (grad, grad, grad),
+        (pieces, own_half(deltas), own_half(hidden)),
+        place,
     )
     result = jnp.stack([output, input_grad])
     result, gate_grad, up_grad, down_grad = lax.optimization_barrier(

time: 278 us -> 272 us (0.978)
  starting transfers between devices: 111 us -> 89.2 us
  blocking collectives: 38.1 us -> 51.1 us
    ppermute x7 -> x0, starting transfers between devices: 32.6 us -> none  [shift(): return lax.ppermute(value, DEPTH, [(i, (i + by) % 16) for i in range(16)])]
    unnamed x2 -> x3, waiting for transfers between devices: 0.03 us -> 32.5 us
    reduce_scatter x1 -> x0, waiting for transfers between devices: 32.4 us -> none  [per_device(): lax.psum_scatter(part.reshape(8 * tok, wide), DEPTH, scatter_dimension=0,...]
    all_to_all x1 -> x2, starting transfers between devices: 6.2 us -> 38.3 us  [reduced(): sums = lax.all_to_all(sums, ('x', 'y', 'c'), 0, 0, tiled=True)]
    all_gather x0 -> x1, blocking collectives: none -> 29.5 us  [per_device(): hidden = lax.all_gather(hidden, DEPTH, axis=0, tiled=True)]
    ppermute x4 -> x2, starting transfers between devices: 27.7 us -> 6.93 us  [swap(): return lax.ppermute(value, axis, [(0, 1), (1, 0)])]
    all_to_all x1 -> x2, waiting for transfers between devices: 0.01 us -> 18.8 us  [reduced(): sums = lax.all_to_all(sums, ('x', 'y', 'c'), 0, 0, tiled=True)]
    all_to_all x1 -> x0, blocking collectives: 16.6 us -> none  [over_plane(): sums = lax.all_to_all(sums, ('x', 'y'), 0, 0, tiled=True)]
  transfers between devices with their start and end apart: 21 -> 13, of which waited for: 11 -> 7; matrix products, arithmetic and copies ran while one was open for 7% -> 8% of each run, Pallas kernels for 1% -> 2%
where the time goes in v4:
time: 272 us; the launch traced here: 271 us
  starting transfers between devices  89.2 us (33%)
  waiting for transfers between devices  74.2 us (27%)
  blocking collectives  51.1 us (19%)
  local copies, waits for them, and re-layouts  26.2 us (10%)
  between operations  14.4 us (5%)
  Pallas kernels  9.09 us (3%)
  other arithmetic  7.16 us (3%)
    all_to_all x2, starting transfers between devices, reduced(): sums = lax.all_to_all(sums, ('x', 'y', 'c'), 0, 0, tiled=True)  38.3 us
    unnamed x3, waiting for transfers between devices  32.5 us
    all_gather x1, blocking collectives, per_device(): hidden = lax.all_gather(hidden, DEPTH, axis=0, tiled=True)  29.5 us
    all_to_all x1, blocking collectives, gather_plane(): own = lax.all_to_all(both, ('x', 'y'), 0, 0, tiled=True)  21.6 us
    all_to_all x2, waiting for transfers between devices, reduced(): sums = lax.all_to_all(sums, ('x', 'y', 'c'), 0, 0, tiled=True)  18.8 us
    ppermute x1, starting transfers between devices, per_device(): near = lax.ppermute(both, ('zh', 'c'), TURN)  16.8 us
    ppermute x1, waiting for transfers between devices, per_device(): far = lax.ppermute(both, ('zh', 'c'), [(0, 2), (1, 0), (2, 3), (3, 1)])  12.1 us
    unnamed x21, local copies, waits for them, and re-layouts  12.1 us
  transfers between devices with their start and end apart: 13, of which 7 were waited for; matrix products, arithmetic and copies ran while one was open for 8% of the time, Pallas kernels for 2%

profile of v4, /device:TPU:1, one launch (start us, length us, event | category | flops | bytes accessed | tf_op | source)
XLA Modules:
  0.0 271.2 jit_solution(14762357091613164748)
XLA Ops:
  8.0 16.8 %collective-permute-start = (bf16[2,128,128]{2,1,0:T(8,128)(2,1)S(1)}, bf16[2,128,128]{2,1,0:T(8,128)(2,1)S(1)}, u32[]{:S(2)}, u32[]{:S(2)}) collective-permute-start(bf16[2,128,128]{2,1,0:T(8,128)(2,1)S(1)} %pad_maximum_fusion.3), channel_id=1, source_target_pairs={{0,0},{8,64},{64,8},{72,72},{1,1},{9,65},{65,9},{73,73},{2,2},{10,... | collective-permute-start | bytes 196616 | tf_op jit(solution)/shard_map/ppermute | solution.py:131
  28.7 6.8 %all-to-all-start = ((bf16[16,2,128,128]{3,2,1,0:T(8,128)(2,1)}), bf16[16,2,128,128]{3,2,1,0:T(8,128)(2,1)S(1)}, u32[]{:S(2)}, u32[]{:S(2)}) async-start(bf16[16,2,128,128]{3,2,1,0:T(8,128)(2,1)} %broadcast_in_dim.26), calls=%async_computation | async-start | bytes 2097152 | tf_op jit(solution)/shard_map/all_to_all | solution.py:110
  36.6 3.3 %collective-permute-start.2 = (bf16[128,1344]{1,0:T(8,128)(2,1)}, bf16[128,1344]{1,0:T(8,128)(2,1)}, u32[]{:S(2)}, u32[]{:S(2)}) collective-permute-start(bf16[128,1344]{1,0:T(8,128)(2,1)} %bitcast.10), channel_id=1, source_target_pairs={{0,128},{128,256},{256,384},{384,0},{1,129},{129,257},{257,385},{3... | collective-permute-start | bytes 1032200 | tf_op jit(solution)/shard_map/ppermute | solution.py:135
  40.8 4.3 %collective-permute-start.3 = (bf16[128,1344]{1,0:T(8,128)(2,1)}, bf16[128,1344]{1,0:T(8,128)(2,1)}, u32[]{:S(2)}, u32[]{:S(2)}) collective-permute-start(bf16[128,1344]{1,0:T(8,128)(2,1)} %bitcast.12), channel_id=1, source_target_pairs={{0,256},{128,384},{256,0},{384,128},{1,257},{129,385},{257,1},{385... | collective-permute-start | bytes 1032200 | tf_op jit(solution)/shard_map/ppermute | solution.py:135
  46.0 3.1 %collective-permute-start.4 = (bf16[128,1344]{1,0:T(8,128)(2,1)}, bf16[128,1344]{1,0:T(8,128)(2,1)}, u32[]{:S(2)}, u32[]{:S(2)}) collective-permute-start(bf16[128,1344]{1,0:T(8,128)(2,1)} %bitcast.14), channel_id=1, source_target_pairs={{0,384},{128,0},{256,128},{384,256},{1,385},{129,1},{257,129},{385... | collective-permute-start | bytes 1032200 | tf_op jit(solution)/shard_map/ppermute | solution.py:135
  58.4 2.5 copy-done
  62.8 12.1 %collective-permute-done.5 = bf16[2,128,128]{2,1,0:T(8,128)(2,1)S(1)} collective-permute-done((bf16[2,128,128]{2,1,0:T(8,128)(2,1)}, bf16[2,128,128]{2,1,0:T(8,128)(2,1)S(1)}, u32[]{:S(2)}, u32[]{:S(2)}) %collective-permute-start.5) | collective-permute-done | bytes 65568 | tf_op jit(solution)/shard_map/ppermute | solution.py:153
  75.2 21.6 %all_to_all.20 = bf16[16,2,128,128]{3,2,1,0:T(8,128)(2,1)S(1)} all-to-all(bf16[16,2,128,128]{3,2,1,0:T(8,128)(2,1)S(1)} %broadcast_in_dim.31), channel_id=1, replica_groups=mesh['x'=4,'zh'=2,'y'=4,'c'=2,'gz'=8] {'x','y'}, dimensions={0} | all-to-all | bytes 2097152 | tf_op jit(solution)/shard_map/all_to_all | solution.py:110
  96.7 5.0 %collective-permute-start.6 = (bf16[4,4,2,128,128]{4,3,2,1,0:T(8,128)(2,1)S(1)}, bf16[4,4,2,128,128]{4,3,2,1,0:T(8,128)(2,1)S(1)}, u32[]{:S(2)}, u32[]{:S(2)}) collective-permute-start(bf16[4,4,2,128,128]{4,3,2,1,0:T(8,128)(2,1)S(1)} %bitcast.53), channel_id=1, source_target_pairs={{0,8},{8,0},{1,9},{9,1},{2,10},{10,2},{3,11},{11,3},{4,12},{12,4},... | collective-permute-start | bytes 3145736 | tf_op jit(solution)/shard_map/ppermute | solution.py:23
  101.7 2.3 collective-permute-done.6
  104.0 2.3 pad_maximum_fusion
  106.3 32.5 %reduce-scatter.4.cloned.1.call-done = f32[64,1344]{1,0:T(8,128)} async-done(((f32[1024,1344]{1,0:T(8,128)}), f32[64,1344]{1,0:T(8,128)}) %reduce-scatter.4.cloned.1.call-update) | async-done | bytes 344080
  141.4 29.5 %all_gather.7 = bf16[1024,448]{1,0:T(8,128)(2,1)S(1)} all-gather(bf16[64,448]{1,0:T(8,128)(2,1)S(1)} %copy.33), channel_id=1, replica_groups=mesh['x'=4,'zh'=2,'y'=4,'c'=2,'gz'=8] {'zh','gz'}, dimensions={0}, use_global_device_ids=true | all-gather | bytes 974848 | tf_op jit(solution)/shard_map/all_gather | solution.py:166
  172.6 22.4 %all-to-all-start.2 = ((bf16[32,128,128]{2,1,0:T(8,128)(2,1)}), bf16[32,128,128]{2,1,0:T(8,128)(2,1)S(1)}, u32[]{:S(2)}, u32[]{:S(2)}) async-start(bf16[32,128,128]{2,1,0:T(8,128)(2,1)} %bitcast.24), calls=%async_computation.2 | async-start | bytes 2097152 | tf_op jit(solution)/shard_map/all_to_all | solution.py:175
  195.1 16.9 %all-to-all-done.2 = bf16[32,128,128]{2,1,0:T(8,128)(2,1)S(1)} async-done(((bf16[32,128,128]{2,1,0:T(8,128)(2,1)}), bf16[32,128,128]{2,1,0:T(8,128)(2,1)S(1)}, u32[]{:S(2)}, u32[]{:S(2)}) %all-to-all-start.2) | async-done | bytes 1048608 | tf_op jit(solution)/shard_map/all_to_all | solution.py:175
  214.3 2.3 shard_map.94
  216.5 15.9 %all-to-all-start.3 = ((bf16[32,128,128]{2,1,0:T(8,128)(2,1)}), bf16[32,128,128]{2,1,0:T(8,128)(2,1)S(1)}, u32[]{:S(2)}, u32[]{:S(2)}) async-start(bf16[32,128,128]{2,1,0:T(8,128)(2,1)} %bitcast.27), calls=%async_computation.3 | async-start | bytes 2097152 | tf_op jit(solution)/shard_map/all_to_all | solution.py:175
  233.7 2.1 copy.46
  235.8 2.0 copy.45
  238.9 2.5 copy.34
  244.2 3.2 %shard_map.95 = (bf16[224,1024]{1,0:T(8,128)(2,1)}, bf16[224,1024]{1,0:T(8,128)(2,1)}, bf16[224,1024]{1,0:T(8,128)(2,1)}) custom-call(s32[2]{0:T(128)S(1)} %pad_add_fusion.place_ref, bf16[2,2,4,4,2,128,128]{6,5,4,3,2,1,0:T(8,128)(2,1)S(1)} %bitcast.46, bf16[448,1024]{1,0:T(8,128)(2,1)S(1)} %maximum_bitcast_fusion.deltas_ref, ...), custom_call_target="tpu_custom_call" | custom-call | tf_op jit(solution)/shard_map/pallas_call | solution.py:98
  247.4 1.9 all-to-all-done.3
  249.5 7.8 %collective-permute-start.7 = (bf16[2,128,128]{2,1,0:T(8,128)(2,1)S(1)}, bf16[2,128,128]{2,1,0:T(8,128)(2,1)S(1)}, u32[]{:S(2)}, u32[]{:S(2)}) collective-permute-start(bf16[2,128,128]{2,1,0:T(8,128)(2,1)S(1)} %pad_maximum_fusion.4), channel_id=1, source_target_pairs={{0,0},{8,64},{64,8},{72,72},{1,1},{9,65},{65,9},{73,73},{2,2},{10,... | collective-permute-start | bytes 196616 | tf_op jit(solution)/shard_map/ppermute | solution.py:206
  257.2 6.5 %collective-permute-done.7 = bf16[2,128,128]{2,1,0:T(8,128)(2,1)S(1)} collective-permute-done((bf16[2,128,128]{2,1,0:T(8,128)(2,1)S(1)}, bf16[2,128,128]{2,1,0:T(8,128)(2,1)S(1)}, u32[]{:S(2)}, u32[]{:S(2)}) %collective-permute-start.7) | collective-permute-done | bytes 65568 | tf_op jit(solution)/shard_map/ppermute | solution.py:206
  (61 shorter events, 31.4 us)
Async XLA Ops:
  7.9 20.7 %copy-start.6 = (bf16[2,128,128]{2,1,0:T(8,128)(2,1)}, bf16[2,128,128]{2,1,0:T(8,128)(2,1)S(1)}, u32[]{:S(2)}) copy-start(bf16[2,128,128]{2,1,0:T(8,128)(2,1)S(1)} %pad_maximum_fusion.3) | copy-start | bytes 196612
  8.0 19.4 %collective-permute-start = (bf16[2,128,128]{2,1,0:T(8,128)(2,1)S(1)}, bf16[2,128,128]{2,1,0:T(8,128)(2,1)S(1)}, u32[]{:S(2)}, u32[]{:S(2)}) collective-permute-start(bf16[2,128,128]{2,1,0:T(8,128)(2,1)S(1)} %pad_maximum_fusion.3), channel_id=1, source_target_pairs={{0,0},{8,64},{64,8},{72,72},{1,1},{9,65},{65,9},{73,73},{2,2},{10,... | collective-permute-start | bytes 196616 | tf_op jit(solution)/shard_map/ppermute | solution.py:131
  27.4 8.1 %copy-start.4 = (bf16[1792,128]{1,0:T(8,128)(2,1)S(1)}, bf16[1792,128]{1,0:T(8,128)(2,1)}, u32[]{:S(2)}) copy-start(bf16[1792,128]{1,0:T(8,128)(2,1)} %param.9) | copy-start | bytes 1376260
  28.7 20.8 %all-to-all-start = ((bf16[16,2,128,128]{3,2,1,0:T(8,128)(2,1)}), bf16[16,2,128,128]{3,2,1,0:T(8,128)(2,1)S(1)}, u32[]{:S(2)}, u32[]{:S(2)}) async-start(bf16[16,2,128,128]{3,2,1,0:T(8,128)(2,1)} %broadcast_in_dim.26), calls=%async_computation | async-start | bytes 2097152 | tf_op jit(solution)/shard_map/all_to_all | solution.py:110
  35.4 103.3 %reduce-scatter.4.cloned.1.call-start = ((), (), s32[]{:S(2)}) async-start(), calls=%async_computation.6 | async-start | bytes 6127616
  36.6 14.8 %collective-permute-start.2 = (bf16[128,1344]{1,0:T(8,128)(2,1)}, bf16[128,1344]{1,0:T(8,128)(2,1)}, u32[]{:S(2)}, u32[]{:S(2)}) collective-permute-start(bf16[128,1344]{1,0:T(8,128)(2,1)} %bitcast.10), channel_id=1, source_target_pairs={{0,128},{128,256},{256,384},{384,0},{1,129},{129,257},{257,385},{3... | collective-permute-start | bytes 1032200 | tf_op jit(solution)/shard_map/ppermute | solution.py:135
  40.8 13.6 %collective-permute-start.3 = (bf16[128,1344]{1,0:T(8,128)(2,1)}, bf16[128,1344]{1,0:T(8,128)(2,1)}, u32[]{:S(2)}, u32[]{:S(2)}) collective-permute-start(bf16[128,1344]{1,0:T(8,128)(2,1)} %bitcast.12), channel_id=1, source_target_pairs={{0,256},{128,384},{256,0},{384,128},{1,257},{129,385},{257,1},{385... | collective-permute-start | bytes 1032200 | tf_op jit(solution)/shard_map/ppermute | solution.py:135
  46.0 9.4 %collective-permute-start.4 = (bf16[128,1344]{1,0:T(8,128)(2,1)}, bf16[128,1344]{1,0:T(8,128)(2,1)}, u32[]{:S(2)}, u32[]{:S(2)}) collective-permute-start(bf16[128,1344]{1,0:T(8,128)(2,1)} %bitcast.14), channel_id=1, source_target_pairs={{0,384},{128,0},{256,128},{384,256},{1,385},{129,1},{257,129},{385... | collective-permute-start | bytes 1032200 | tf_op jit(solution)/shard_map/ppermute | solution.py:135
  49.5 6.9 %collective-permute-start.1 = (bf16[4,4,2,128,128]{4,3,2,1,0:T(8,128)(2,1)S(1)}, bf16[4,4,2,128,128]{4,3,2,1,0:T(8,128)(2,1)S(1)}, u32[]{:S(2)}, u32[]{:S(2)}) collective-permute-start(bf16[4,4,2,128,128]{4,3,2,1,0:T(8,128)(2,1)S(1)} %bitcast.48), channel_id=1, source_target_pairs={{0,8},{8,0},{1,9},{9,1},{2,10},{10,2},{3,11},{11,3},{4,12},{12,4},... | collective-permute-start | bytes 3145736 | tf_op jit(solution)/shard_map/ppermute | solution.py:23
  58.3 2.5 copy-start
  60.8 151.9 %all-gather.2.cloned.1.call-start = ((), (), s32[]{:S(2)}) async-start(), calls=%async_computation.5 | async-start | bytes 1949696 | tf_op jit(solution)/shard_map/all_gather | solution.py:165
  60.9 14.0 %collective-permute-start.5 = (bf16[2,128,128]{2,1,0:T(8,128)(2,1)}, bf16[2,128,128]{2,1,0:T(8,128)(2,1)S(1)}, u32[]{:S(2)}, u32[]{:S(2)}) collective-permute-start(bf16[2,128,128]{2,1,0:T(8,128)(2,1)} %copy-done.6), channel_id=1, source_target_pairs={{0,64},{8,0},{64,72},{72,8},{1,65},{9,1},{65,73},{73,9},{2,66},{10... | collective-permute-start | bytes 196616 | tf_op jit(solution)/shard_map/ppermute | solution.py:153
  96.7 7.3 %collective-permute-start.6 = (bf16[4,4,2,128,128]{4,3,2,1,0:T(8,128)(2,1)S(1)}, bf16[4,4,2,128,128]{4,3,2,1,0:T(8,128)(2,1)S(1)}, u32[]{:S(2)}, u32[]{:S(2)}) collective-permute-start(bf16[4,4,2,128,128]{4,3,2,1,0:T(8,128)(2,1)S(1)} %bitcast.53), channel_id=1, source_target_pairs={{0,8},{8,0},{1,9},{9,1},{2,10},{10,2},{3,11},{11,3},{4,12},{12,4},... | collective-permute-start | bytes 3145736 | tf_op jit(solution)/shard_map/ppermute | solution.py:23
  172.6 39.4 %all-to-all-start.2 = ((bf16[32,128,128]{2,1,0:T(8,128)(2,1)}), bf16[32,128,128]{2,1,0:T(8,128)(2,1)S(1)}, u32[]{:S(2)}, u32[]{:S(2)}) async-start(bf16[32,128,128]{2,1,0:T(8,128)(2,1)} %bitcast.24), calls=%async_computation.2 | async-start | bytes 2097152 | tf_op jit(solution)/shard_map/all_to_all | solution.py:175
  212.8 1.5 copy-start.2
  216.5 32.8 %all-to-all-start.3 = ((bf16[32,128,128]{2,1,0:T(8,128)(2,1)}), bf16[32,128,128]{2,1,0:T(8,128)(2,1)S(1)}, u32[]{:S(2)}, u32[]{:S(2)}) async-start(bf16[32,128,128]{2,1,0:T(8,128)(2,1)} %bitcast.27), calls=%async_computation.3 | async-start | bytes 2097152 | tf_op jit(solution)/shard_map/all_to_all | solution.py:175
  233.7 5.2 %copy-start.3 = (bf16[1024,896]{1,0:T(8,128)(2,1)S(1)}, bf16[1024,896]{1,0:T(8,128)(2,1)}, u32[]{:S(2)}) copy-start(bf16[1024,896]{1,0:T(8,128)(2,1)} %all-gather.2.cloned.1.call-done) | copy-start | bytes 5505028
  241.4 2.7 %copy-start.1 = (bf16[4,4,4,2,128,128]{5,4,3,2,1,0:T(8,128)(2,1)S(1)}, bf16[4,4,4,2,128,128]{5,4,3,2,1,0:T(8,128)(2,1)}, u32[]{:S(2)}) copy-start(bf16[4,4,4,2,128,128]{5,4,3,2,1,0:T(8,128)(2,1)} %pad_maximum_fusion) | copy-start | bytes 12582916
  244.2 5.3 %copy-start.5 = (bf16[128,128]{1,0:T(8,128)(2,1)S(1)}, bf16[128,128]{1,0:T(8,128)(2,1)}, u32[]{:S(2)}) copy-start(bf16[128,128]{1,0:T(8,128)(2,1)} %reduce_sum.24) | copy-start | bytes 98308
  249.5 14.3 %collective-permute-start.7 = (bf16[2,128,128]{2,1,0:T(8,128)(2,1)S(1)}, bf16[2,128,128]{2,1,0:T(8,128)(2,1)S(1)}, u32[]{:S(2)}, u32[]{:S(2)}) collective-permute-start(bf16[2,128,128]{2,1,0:T(8,128)(2,1)S(1)} %pad_maximum_fusion.4), channel_id=1, source_target_pairs={{0,0},{8,64},{64,8},{72,72},{1,1},{9,65},{65,9},{73,73},{2,2},{10,... | collective-permute-start | bytes 196616 | tf_op jit(solution)/shard_map/ppermute | solution.py:206
Sparse Core Ops, SparseCore 0:
  61.0 77.7 reduce-scatter.3
  141.4 70.2 all-gather.1

commit v5 on v4

--- a/solution.py
+++ b/solution.py
@@ -191,20 +191,20 @@
         ).T
 
     output = reduced(hidden, 2 * cols)
-    deltas, output = lax.optimization_barrier((deltas, output))
+    hidden = own_half(hidden)
+    deltas, output, hidden = lax.optimization_barrier((deltas, output, hidden))
+    output = lax.ppermute(output, ("zh", "c"), TURN)
     input_grad = reduced(deltas, 0)
-    gate_grad, up_grad, down_grad = local_call(
+    grads = local_call(
         grads_kernel,
         (grad, grad, grad),
-        (pieces, own_half(deltas), own_half(hidden)),
+        (pieces, own_half(deltas), hidden),
         place,
     )
-    result = jnp.stack([output, input_grad])
-    result, gate_grad, up_grad, down_grad = lax.optimization_barrier(
-        (result, gate_grad, up_grad, down_grad)
-    )
-    result = lax.ppermute(result, ("zh", "c"), TURN)
-    return result[0], result[1], gate_grad.T, up_grad.T, down_grad
+    input_grad, grads = lax.optimization_barrier((input_grad, grads))
+    gate_grad, up_grad, down_grad = grads
+    input_grad = lax.ppermute(input_grad, ("zh", "c"), TURN)
+    return output, input_grad, gate_grad.T, up_grad.T, down_grad
 
 
 def solution(mesh):

time: 272 us -> 273 us (level)
  starting transfers between devices: 89.2 us -> 98.3 us
  waiting for transfers between devices: 74.2 us -> 66.8 us
    ppermute x1 -> x2, starting transfers between devices: 7.76 us -> 15.7 us  [the longest x1 8.05 us: per_device(): output = lax.ppermute(output, ('zh', 'c'), TURN)]
    all_to_all x2, waiting for transfers between devices: 18.8 us -> 12.1 us  [reduced(): sums = lax.all_to_all(sums, ('x', 'y', 'c'), 0, 0, tiled=True)]
    ppermute x1 -> x2, waiting for transfers between devices: 6.53 us -> 6.24 us  [the longest x1 6.23 us: per_device(): input_grad = lax.ppermute(input_grad, ('zh', 'c'), TURN)]
    unnamed x21 -> x23, local copies, waits for them, and re-layouts: 12.1 us -> 12.2 us
  transfers between devices with their start and end apart: 13 -> 14, of which waited for: 7 -> 7; matrix products, arithmetic and copies ran while one was open for 8% -> 8% of each run, Pallas kernels for 2% -> 2%
where the time goes in v5:
time: 273 us; the launch traced here: 272 us
  starting transfers between devices  98.3 us (36%)
  waiting for transfers between devices  66.8 us (24%)
  blocking collectives  50.6 us (19%)
  local copies, waits for them, and re-layouts  25.6 us (9%)
  between operations  14.4 us (5%)
  Pallas kernels  9.05 us (3%)
  other arithmetic  7.03 us (3%)
    all_to_all x2, starting transfers between devices, reduced(): sums = lax.all_to_all(sums, ('x', 'y', 'c'), 0, 0, tiled=True)  39.4 us
    unnamed x3, waiting for transfers between devices  32.2 us
    all_gather x1, blocking collectives, per_device(): hidden = lax.all_gather(hidden, DEPTH, axis=0, tiled=True)  29 us
    all_to_all x1, blocking collectives, gather_plane(): own = lax.all_to_all(both, ('x', 'y'), 0, 0, tiled=True)  21.6 us
    ppermute x1, starting transfers between devices, per_device(): near = lax.ppermute(both, ('zh', 'c'), TURN)  16.8 us
    unnamed x23, local copies, waits for them, and re-layouts  12.2 us
    ppermute x1, waiting for transfers between devices, per_device(): far = lax.ppermute(both, ('zh', 'c'), [(0, 2), (1, 0), (2, 3), (3, 1)])  12.1 us
    all_to_all x2, waiting for transfers between devices, reduced(): sums = lax.all_to_all(sums, ('x', 'y', 'c'), 0, 0, tiled=True)  12.1 us
  transfers between devices with their start and end apart: 14, of which 7 were waited for; matrix products, arithmetic and copies ran while one was open for 8% of the time, Pallas kernels for 2%

profile of v5, /device:TPU:1, one launch (start us, length us, event | category | flops | bytes accessed | tf_op | source)
XLA Modules:
  0.0 271.8 jit_solution(15851752437136005638)
XLA Ops:
  8.0 16.8 %collective-permute-start = (bf16[2,128,128]{2,1,0:T(8,128)(2,1)S(1)}, bf16[2,128,128]{2,1,0:T(8,128)(2,1)S(1)}, u32[]{:S(2)}, u32[]{:S(2)}) collective-permute-start(bf16[2,128,128]{2,1,0:T(8,128)(2,1)S(1)} %pad_maximum_fusion.3), channel_id=1, source_target_pairs={{0,0},{8,64},{64,8},{72,72},{1,1},{9,65},{65,9},{73,73},{2,2},{10,... | collective-permute-start | bytes 196616 | tf_op jit(solution)/shard_map/ppermute | solution.py:131
  28.7 6.8 %all-to-all-start = ((bf16[16,2,128,128]{3,2,1,0:T(8,128)(2,1)}), bf16[16,2,128,128]{3,2,1,0:T(8,128)(2,1)S(1)}, u32[]{:S(2)}, u32[]{:S(2)}) async-start(bf16[16,2,128,128]{3,2,1,0:T(8,128)(2,1)} %broadcast_in_dim.26), calls=%async_computation | async-start | bytes 2097152 | tf_op jit(solution)/shard_map/all_to_all | solution.py:110
  36.6 3.3 %collective-permute-start.2 = (bf16[128,1344]{1,0:T(8,128)(2,1)}, bf16[128,1344]{1,0:T(8,128)(2,1)}, u32[]{:S(2)}, u32[]{:S(2)}) collective-permute-start(bf16[128,1344]{1,0:T(8,128)(2,1)} %bitcast.10), channel_id=1, source_target_pairs={{0,128},{128,256},{256,384},{384,0},{1,129},{129,257},{257,385},{3... | collective-permute-start | bytes 1032200 | tf_op jit(solution)/shard_map/ppermute | solution.py:135
  40.8 4.3 %collective-permute-start.3 = (bf16[128,1344]{1,0:T(8,128)(2,1)}, bf16[128,1344]{1,0:T(8,128)(2,1)}, u32[]{:S(2)}, u32[]{:S(2)}) collective-permute-start(bf16[128,1344]{1,0:T(8,128)(2,1)} %bitcast.12), channel_id=1, source_target_pairs={{0,256},{128,384},{256,0},{384,128},{1,257},{129,385},{257,1},{385... | collective-permute-start | bytes 1032200 | tf_op jit(solution)/shard_map/ppermute | solution.py:135
  46.0 3.1 %collective-permute-start.4 = (bf16[128,1344]{1,0:T(8,128)(2,1)}, bf16[128,1344]{1,0:T(8,128)(2,1)}, u32[]{:S(2)}, u32[]{:S(2)}) collective-permute-start(bf16[128,1344]{1,0:T(8,128)(2,1)} %bitcast.14), channel_id=1, source_target_pairs={{0,384},{128,0},{256,128},{384,256},{1,385},{129,1},{257,129},{385... | collective-permute-start | bytes 1032200 | tf_op jit(solution)/shard_map/ppermute | solution.py:135
  58.4 2.5 copy-done
  62.8 12.1 %collective-permute-done.5 = bf16[2,128,128]{2,1,0:T(8,128)(2,1)S(1)} collective-permute-done((bf16[2,128,128]{2,1,0:T(8,128)(2,1)}, bf16[2,128,128]{2,1,0:T(8,128)(2,1)S(1)}, u32[]{:S(2)}, u32[]{:S(2)}) %collective-permute-start.5) | collective-permute-done | bytes 65568 | tf_op jit(solution)/shard_map/ppermute | solution.py:153
  75.2 21.6 %all_to_all.20 = bf16[16,2,128,128]{3,2,1,0:T(8,128)(2,1)S(1)} all-to-all(bf16[16,2,128,128]{3,2,1,0:T(8,128)(2,1)S(1)} %broadcast_in_dim.31), channel_id=1, replica_groups=mesh['x'=4,'zh'=2,'y'=4,'c'=2,'gz'=8] {'x','y'}, dimensions={0} | all-to-all | bytes 2097152 | tf_op jit(solution)/shard_map/all_to_all | solution.py:110
  96.7 5.0 %collective-permute-start.6 = (bf16[4,4,2,128,128]{4,3,2,1,0:T(8,128)(2,1)S(1)}, bf16[4,4,2,128,128]{4,3,2,1,0:T(8,128)(2,1)S(1)}, u32[]{:S(2)}, u32[]{:S(2)}) collective-permute-start(bf16[4,4,2,128,128]{4,3,2,1,0:T(8,128)(2,1)S(1)} %bitcast.47), channel_id=1, source_target_pairs={{0,8},{8,0},{1,9},{9,1},{2,10},{10,2},{3,11},{11,3},{4,12},{12,4},... | collective-permute-start | bytes 3145736 | tf_op jit(solution)/shard_map/ppermute | solution.py:23
  101.7 2.3 collective-permute-done.6
  104.0 2.3 pad_maximum_fusion
  106.3 32.2 %reduce-scatter.4.cloned.1.call-done = f32[64,1344]{1,0:T(8,128)} async-done(((f32[1024,1344]{1,0:T(8,128)}), f32[64,1344]{1,0:T(8,128)}) %reduce-scatter.4.cloned.1.call-update) | async-done | bytes 344080
  141.1 29.0 %all_gather.7 = bf16[1024,448]{1,0:T(8,128)(2,1)S(1)} all-gather(bf16[64,448]{1,0:T(8,128)(2,1)S(1)} %copy.33), channel_id=1, replica_groups=mesh['x'=4,'zh'=2,'y'=4,'c'=2,'gz'=8] {'zh','gz'}, dimensions={0}, use_global_device_ids=true | all-gather | bytes 974848 | tf_op jit(solution)/shard_map/all_gather | solution.py:166
  171.9 23.7 %all-to-all-start.2 = ((bf16[32,128,128]{2,1,0:T(8,128)(2,1)}), bf16[32,128,128]{2,1,0:T(8,128)(2,1)S(1)}, u32[]{:S(2)}, u32[]{:S(2)}) async-start(bf16[32,128,128]{2,1,0:T(8,128)(2,1)} %bitcast.24), calls=%async_computation.2 | async-start | bytes 2097152 | tf_op jit(solution)/shard_map/all_to_all | solution.py:175
  196.8 2.0 copy.46
  198.8 2.0 copy.45
  201.9 10.6 %all-to-all-done.2 = bf16[32,128,128]{2,1,0:T(8,128)(2,1)S(1)} async-done(((bf16[32,128,128]{2,1,0:T(8,128)(2,1)}), bf16[32,128,128]{2,1,0:T(8,128)(2,1)S(1)}, u32[]{:S(2)}, u32[]{:S(2)}) %all-to-all-start.2) | async-done | bytes 1048608 | tf_op jit(solution)/shard_map/all_to_all | solution.py:175
  214.8 2.3 shard_map.94
  217.0 15.7 %all-to-all-start.3 = ((bf16[32,128,128]{2,1,0:T(8,128)(2,1)}), bf16[32,128,128]{2,1,0:T(8,128)(2,1)S(1)}, u32[]{:S(2)}, u32[]{:S(2)}) async-start(bf16[32,128,128]{2,1,0:T(8,128)(2,1)} %bitcast.27), calls=%async_computation.3 | async-start | bytes 2097152 | tf_op jit(solution)/shard_map/all_to_all | solution.py:175
  232.8 2.5 copy.36
  235.4 8.0 %collective-permute-start.7 = (bf16[128,128]{1,0:T(8,128)(2,1)S(1)}, bf16[128,128]{1,0:T(8,128)(2,1)S(1)}, u32[]{:S(2)}, u32[]{:S(2)}) collective-permute-start(bf16[128,128]{1,0:T(8,128)(2,1)S(1)} %copy-done.6), channel_id=1, source_target_pairs={{0,0},{8,64},{64,8},{72,72},{1,1},{9,65},{65,9},{73,73},{2,2},{10,... | collective-permute-start | bytes 98312 | tf_op jit(solution)/shard_map/ppermute | solution.py:196
  245.0 3.2 %shard_map.95 = (bf16[224,1024]{1,0:T(8,128)(2,1)}, bf16[224,1024]{1,0:T(8,128)(2,1)}, bf16[224,1024]{1,0:T(8,128)(2,1)}) custom-call(s32[2]{0:T(128)S(1)} %pad_add_fusion.place_ref, bf16[2,2,4,4,2,128,128]{6,5,4,3,2,1,0:T(8,128)(2,1)S(1)} %bitcast.40, bf16[448,1024]{1,0:T(8,128)(2,1)S(1)} %maximum_bitcast_fusion.deltas_ref, ...), custom_call_target="tpu_custom_call" | custom-call | tf_op jit(solution)/shard_map/pallas_call | solution.py:98
  249.8 7.7 %collective-permute-start.8 = (bf16[128,128]{1,0:T(8,128)(2,1)S(1)}, bf16[128,128]{1,0:T(8,128)(2,1)S(1)}, u32[]{:S(2)}, u32[]{:S(2)}) collective-permute-start(bf16[128,128]{1,0:T(8,128)(2,1)S(1)} %reduce_sum.25), channel_id=1, source_target_pairs={{0,0},{8,64},{64,8},{72,72},{1,1},{9,65},{65,9},{73,73},{2,2},{10,... | collective-permute-start | bytes 98312 | tf_op jit(solution)/shard_map/ppermute | solution.py:206
  257.5 6.2 %collective-permute-done.8 = bf16[128,128]{1,0:T(8,128)(2,1)S(1)} collective-permute-done((bf16[128,128]{1,0:T(8,128)(2,1)S(1)}, bf16[128,128]{1,0:T(8,128)(2,1)S(1)}, u32[]{:S(2)}, u32[]{:S(2)}) %collective-permute-start.8) | collective-permute-done | bytes 32800 | tf_op jit(solution)/shard_map/ppermute | solution.py:206
  (63 shorter events, 32.4 us)
Async XLA Ops:
  7.9 20.7 %copy-start.5 = (bf16[2,128,128]{2,1,0:T(8,128)(2,1)}, bf16[2,128,128]{2,1,0:T(8,128)(2,1)S(1)}, u32[]{:S(2)}) copy-start(bf16[2,128,128]{2,1,0:T(8,128)(2,1)S(1)} %pad_maximum_fusion.3) | copy-start | bytes 196612
  8.0 19.4 %collective-permute-start = (bf16[2,128,128]{2,1,0:T(8,128)(2,1)S(1)}, bf16[2,128,128]{2,1,0:T(8,128)(2,1)S(1)}, u32[]{:S(2)}, u32[]{:S(2)}) collective-permute-start(bf16[2,128,128]{2,1,0:T(8,128)(2,1)S(1)} %pad_maximum_fusion.3), channel_id=1, source_target_pairs={{0,0},{8,64},{64,8},{72,72},{1,1},{9,65},{65,9},{73,73},{2,2},{10,... | collective-permute-start | bytes 196616 | tf_op jit(solution)/shard_map/ppermute | solution.py:131
  27.4 8.1 %copy-start.4 = (bf16[1792,128]{1,0:T(8,128)(2,1)S(1)}, bf16[1792,128]{1,0:T(8,128)(2,1)}, u32[]{:S(2)}) copy-start(bf16[1792,128]{1,0:T(8,128)(2,1)} %param.9) | copy-start | bytes 1376260
  28.7 20.8 %all-to-all-start = ((bf16[16,2,128,128]{3,2,1,0:T(8,128)(2,1)}), bf16[16,2,128,128]{3,2,1,0:T(8,128)(2,1)S(1)}, u32[]{:S(2)}, u32[]{:S(2)}) async-start(bf16[16,2,128,128]{3,2,1,0:T(8,128)(2,1)} %broadcast_in_dim.26), calls=%async_computation | async-start | bytes 2097152 | tf_op jit(solution)/shard_map/all_to_all | solution.py:110
  35.4 103.0 %reduce-scatter.4.cloned.1.call-start = ((), (), s32[]{:S(2)}) async-start(), calls=%async_computation.6 | async-start | bytes 6127616
  36.6 14.8 %collective-permute-start.2 = (bf16[128,1344]{1,0:T(8,128)(2,1)}, bf16[128,1344]{1,0:T(8,128)(2,1)}, u32[]{:S(2)}, u32[]{:S(2)}) collective-permute-start(bf16[128,1344]{1,0:T(8,128)(2,1)} %bitcast.10), channel_id=1, source_target_pairs={{0,128},{128,256},{256,384},{384,0},{1,129},{129,257},{257,385},{3... | collective-permute-start | bytes 1032200 | tf_op jit(solution)/shard_map/ppermute | solution.py:135
  40.8 13.6 %collective-permute-start.3 = (bf16[128,1344]{1,0:T(8,128)(2,1)}, bf16[128,1344]{1,0:T(8,128)(2,1)}, u32[]{:S(2)}, u32[]{:S(2)}) collective-permute-start(bf16[128,1344]{1,0:T(8,128)(2,1)} %bitcast.12), channel_id=1, source_target_pairs={{0,256},{128,384},{256,0},{384,128},{1,257},{129,385},{257,1},{385... | collective-permute-start | bytes 1032200 | tf_op jit(solution)/shard_map/ppermute | solution.py:135
  46.0 9.4 %collective-permute-start.4 = (bf16[128,1344]{1,0:T(8,128)(2,1)}, bf16[128,1344]{1,0:T(8,128)(2,1)}, u32[]{:S(2)}, u32[]{:S(2)}) collective-permute-start(bf16[128,1344]{1,0:T(8,128)(2,1)} %bitcast.14), channel_id=1, source_target_pairs={{0,384},{128,0},{256,128},{384,256},{1,385},{129,1},{257,129},{385... | collective-permute-start | bytes 1032200 | tf_op jit(solution)/shard_map/ppermute | solution.py:135
  49.5 6.9 %collective-permute-start.1 = (bf16[4,4,2,128,128]{4,3,2,1,0:T(8,128)(2,1)S(1)}, bf16[4,4,2,128,128]{4,3,2,1,0:T(8,128)(2,1)S(1)}, u32[]{:S(2)}, u32[]{:S(2)}) collective-permute-start(bf16[4,4,2,128,128]{4,3,2,1,0:T(8,128)(2,1)S(1)} %bitcast.42), channel_id=1, source_target_pairs={{0,8},{8,0},{1,9},{9,1},{2,10},{10,2},{3,11},{11,3},{4,12},{12,4},... | collective-permute-start | bytes 3145736 | tf_op jit(solution)/shard_map/ppermute | solution.py:23
  58.3 2.5 copy-start
  60.8 152.4 %all-gather.2.cloned.1.call-start = ((), (), s32[]{:S(2)}) async-start(), calls=%async_computation.5 | async-start | bytes 1949696 | tf_op jit(solution)/shard_map/all_gather | solution.py:165
  60.9 14.0 %collective-permute-start.5 = (bf16[2,128,128]{2,1,0:T(8,128)(2,1)}, bf16[2,128,128]{2,1,0:T(8,128)(2,1)S(1)}, u32[]{:S(2)}, u32[]{:S(2)}) collective-permute-start(bf16[2,128,128]{2,1,0:T(8,128)(2,1)} %copy-done.5), channel_id=1, source_target_pairs={{0,64},{8,0},{64,72},{72,8},{1,65},{9,1},{65,73},{73,9},{2,66},{10... | collective-permute-start | bytes 196616 | tf_op jit(solution)/shard_map/ppermute | solution.py:153
  96.7 7.3 %collective-permute-start.6 = (bf16[4,4,2,128,128]{4,3,2,1,0:T(8,128)(2,1)S(1)}, bf16[4,4,2,128,128]{4,3,2,1,0:T(8,128)(2,1)S(1)}, u32[]{:S(2)}, u32[]{:S(2)}) collective-permute-start(bf16[4,4,2,128,128]{4,3,2,1,0:T(8,128)(2,1)S(1)} %bitcast.47), channel_id=1, source_target_pairs={{0,8},{8,0},{1,9},{9,1},{2,10},{10,2},{3,11},{11,3},{4,12},{12,4},... | collective-permute-start | bytes 3145736 | tf_op jit(solution)/shard_map/ppermute | solution.py:23
  171.9 40.6 %all-to-all-start.2 = ((bf16[32,128,128]{2,1,0:T(8,128)(2,1)}), bf16[32,128,128]{2,1,0:T(8,128)(2,1)S(1)}, u32[]{:S(2)}, u32[]{:S(2)}) async-start(bf16[32,128,128]{2,1,0:T(8,128)(2,1)} %bitcast.24), calls=%async_computation.2 | async-start | bytes 2097152 | tf_op jit(solution)/shard_map/all_to_all | solution.py:175
  213.3 1.5 copy-start.2
  217.0 15.8 %copy-start.3 = (bf16[1024,896]{1,0:T(8,128)(2,1)S(1)}, bf16[1024,896]{1,0:T(8,128)(2,1)}, u32[]{:S(2)}) copy-start(bf16[1024,896]{1,0:T(8,128)(2,1)} %all-gather.2.cloned.1.call-done) | copy-start | bytes 5505028
  217.0 32.6 %all-to-all-start.3 = ((bf16[32,128,128]{2,1,0:T(8,128)(2,1)}), bf16[32,128,128]{2,1,0:T(8,128)(2,1)S(1)}, u32[]{:S(2)}, u32[]{:S(2)}) async-start(bf16[32,128,128]{2,1,0:T(8,128)(2,1)} %bitcast.27), calls=%async_computation.3 | async-start | bytes 2097152 | tf_op jit(solution)/shard_map/all_to_all | solution.py:175
  232.8 2.5 copy-start.6
  235.4 9.7 %copy-start.1 = (bf16[4,4,4,2,128,128]{5,4,3,2,1,0:T(8,128)(2,1)S(1)}, bf16[4,4,4,2,128,128]{5,4,3,2,1,0:T(8,128)(2,1)}, u32[]{:S(2)}) copy-start(bf16[4,4,4,2,128,128]{5,4,3,2,1,0:T(8,128)(2,1)} %pad_maximum_fusion) | copy-start | bytes 12582916
  235.4 22.2 %collective-permute-start.7 = (bf16[128,128]{1,0:T(8,128)(2,1)S(1)}, bf16[128,128]{1,0:T(8,128)(2,1)S(1)}, u32[]{:S(2)}, u32[]{:S(2)}) collective-permute-start(bf16[128,128]{1,0:T(8,128)(2,1)S(1)} %copy-done.6), channel_id=1, source_target_pairs={{0,0},{8,64},{64,8},{72,72},{1,1},{9,65},{65,9},{73,73},{2,2},{10,... | collective-permute-start | bytes 98312 | tf_op jit(solution)/shard_map/ppermute | solution.py:196
  249.8 13.9 %collective-permute-start.8 = (bf16[128,128]{1,0:T(8,128)(2,1)S(1)}, bf16[128,128]{1,0:T(8,128)(2,1)S(1)}, u32[]{:S(2)}, u32[]{:S(2)}) collective-permute-start(bf16[128,128]{1,0:T(8,128)(2,1)S(1)} %reduce_sum.25), channel_id=1, source_target_pairs={{0,0},{8,64},{64,8},{72,72},{1,1},{9,65},{65,9},{73,73},{2,2},{10,... | collective-permute-start | bytes 98312 | tf_op jit(solution)/shard_map/ppermute | solution.py:206
Sparse Core Ops, SparseCore 0:
  61.0 77.4 reduce-scatter.3
  141.1 71.3 all-gather.1
